TPU v7x, 256 devices: a whole 4x4x8 slice. The times are simulated.
256 devices in a mesh: dp: 16 (over z_hi, y), shard: 16 (over x, z_lo, core).
Axes of the slice: x: 4, y: 4, z: 8 (z_hi: 4, z_lo: 2; z = z_hi * 2 + z_lo), core: 2. Of those that a mesh axis runs over, the one named last changes fastest.
Arguments:
- tokens: bfloat16 [6144, 2048], P('dp', 'shard'), may hold values from -6 to 6
- cotangent: bfloat16 [6144, 2048], P('dp', 'shard'), may hold values from -6 to 6
- route_probs: float32 [6144], P('dp'), may hold values from 0.2 to 1
- w_gate: bfloat16 [2, 2048, 8192], P(None, 'dp', 'shard'), may hold values from -0.125 to 0.125
- w_up: bfloat16 [2, 2048, 8192], P(None, 'dp', 'shard'), may hold values from -0.125 to 0.125
- w_down: bfloat16 [2, 8192, 2048], P(None, 'shard', 'dp'), may hold values from -0.0625 to 0.0625
- tile_counts: int32 [16, 2], P('dp'), may hold values from 0 to 3, as said below
Outputs:
- layer_out: bfloat16 [6144, 2048], P('dp', 'shard')
- prob_grad: float32 [6144], P('dp')
- input_grad: bfloat16 [6144, 2048], P('dp', 'shard')
- gate_grad: bfloat16 [2, 2048, 8192], P(None, 'dp', 'shard')
- up_grad: bfloat16 [2, 2048, 8192], P(None, 'dp', 'shard')
- down_grad: bfloat16 [2, 8192, 2048], P(None, 'shard', 'dp')
Inputs may be any that keep to these rules, and one draw needn't show every extreme that they name: `tile_counts`: each group's counts sum to at most 3 and at least 1; in every draw some group has all 3 slots of one expert.
All inputs are finite; a program needn't handle non-finite values.
Results may differ from a plain program's by a relative error of at most 0.023.
Values may be sent and summed in bfloat16 or wider, within the bound.
No kernel may reach another device: no remote copies, remote signals or barrier semaphores. Data moves between devices by JAX's collectives and lax.ppermute only.
A program may use at most 128 MiB of HBM per device.

v0:
```python
import jax
import jax.numpy as jnp
from jax import lax
from jax.experimental import pallas as pl
from jax.experimental.pallas import tpu as pltpu
from jax.sharding import Mesh, PartitionSpec as P

TILE = 128
ROWS = 384
F32 = jnp.float32
BF16 = jnp.bfloat16
SIZES = {"zh": 4, "y": 4, "x": 4, "zl": 2, "c": 2}
VMEM = pl.BlockSpec(memory_space=pltpu.VMEM)
SMEM = pl.BlockSpec(memory_space=pltpu.SMEM)


def call(kernel, outs, n_smem, args, scratch=(), deps=(), flops=0, nbytes=0):
    n, m = len(args), len(deps)

    def body(*refs):
        kernel(*refs[:n], *refs[n + m :])

    return pl.pallas_call(
        body,
        out_shape=[jax.ShapeDtypeStruct(s, d) for s, d in outs],
        in_specs=[SMEM] * n_smem
        + [VMEM] * (n - n_smem)
        + [pl.BlockSpec(memory_space=pl.ANY)] * m,
        out_specs=[VMEM] * len(outs),
        scratch_shapes=list(scratch),
        compiler_params=pltpu.CompilerParams(vmem_limit_bytes=56 * 2**20),
        cost_estimate=pl.CostEstimate(
            flops=flops, bytes_accessed=nbytes, transcendentals=0
        ),
        name=kernel.__name__,
    )(*args, *deps)


def shift(v, axis, by):
    n = SIZES[axis]
    return lax.ppermute(v, axis, [(i, (i + by) % n) for i in range(n)])


def to_core(v, k):
    pairs = []
    for zh in range(4):
        for c in range(2):
            a, b = divmod(zh, 2)
            pairs.append((zh * 2 + c, ((2 * b + c + k) % 4) * 2 + a))
    return lax.ppermute(v, ("zh", "c"), pairs)


def from_core(v, k):
    pairs = []
    for zh in range(4):
        for c in range(2):
            a, b = divmod(zh, 2)
            pairs.append((((2 * b + c + k) % 4) * 2 + a, zh * 2 + c))
    return lax.ppermute(v, ("zh", "c"), pairs)


def ring(v, axis):
    half = v.shape[0] // 2
    before = shift(v, axis, 1)
    after = shift(v, axis, 3)
    return [v, before, after, shift(before[:half], axis, 1), shift(after[half:], axis, 3)]


def mod4(v):
    return lax.rem(v + 4, 4)


def dot(a, b, dims):
    return lax.dot_general(a, b, (dims, ((), ())), preferred_element_type=F32)


def pack_tokens(counts, tok, cot, prob, msg):
    msg[0:ROWS] = tok[...]
    msg[ROWS : 2 * ROWS] = (prob[...] * cot[...].astype(F32)).astype(BF16)
    one = jnp.ones((8, 128), F32)
    tile = jnp.concatenate(
        [one * counts[0, 0].astype(F32), one * counts[0, 1].astype(F32)], axis=0
    )
    msg[2 * ROWS : 2 * ROWS + 16] = tile.astype(BF16)


def pack_weights(pos, wg, wu, wd, w0, w1, w2, w3):
    for k, out in enumerate((w0, w1, w2, w3)):
        q = pl.multiple_of(mod4(pos[0] + k) * 128, 128)
        for e in range(2):
            out[e * 3] = wg[e, :, pl.ds(q, 128)]
            out[e * 3 + 1] = wu[e, :, pl.ds(q, 128)]
            out[e * 3 + 2] = wd[e, pl.ds(q, 128), :]


def place_rows(pos, pieces, base, dst):
    zh, x, zl = pos[0], pos[2], pos[3]
    own, before, after, far_a, far_b = pieces
    for hop, zlrel, ref, lead in (
        (0, 0, own, 0),
        (0, 1, own, 1),
        (3, 0, before, 0),
        (3, 1, before, 1),
        (1, 0, after, 0),
        (1, 1, after, 1),
        (2, 0, far_a, 0),
        (2, 1, far_b, 0),
    ):
        xs = mod4(x + hop)
        zs = lax.rem(zl + zlrel, 2)
        for k in range(4):
            s = mod4(zh - k)
            b, cs = lax.div(s, 2), lax.rem(s, 2)
            col = pl.multiple_of((xs * 4 + zs * 2 + cs) * 128, 128)
            row = pl.multiple_of(b * ROWS, 128)
            at = (lead * 4 + k) * (2 * ROWS + 16) + base
            dst[pl.ds(row, ROWS), pl.ds(col, 128)] = ref[at : at + ROWS, :]


def place_weights(pos, own, other, wgu, wd):
    zh, y = pos[0], pos[1]
    for cs, pieces in enumerate((own, other)):
        a, before, after, far_a, far_b = pieces
        for hop, ref, ks in (
            (0, a, range(4)),
            (3, before, range(4)),
            (1, after, range(4)),
            (2, far_a, range(2)),
            (2, far_b, range(2, 4)),
        ):
            for i, k in enumerate(ks):
                d = pl.multiple_of((mod4(zh - k) * 4 + mod4(y + hop)) * 128, 128)
                for e in range(2):
                    for m in range(2):
                        col = (e * 4 + m * 2 + cs) * 128
                        wgu[pl.ds(d, 128), col : col + 128] = ref[i, e * 3 + m]
                    row = (e * 2 + cs) * 128
                    wd[row : row + 128, pl.ds(d, 128)] = ref[i, e * 3 + 2]


def forward_kernel(*refs):
    pos, cnt, x = refs[:3]
    wo, wx = refs[3:8], refs[8:13]
    wgu, wd, gate_out, up_out, mask, hid, part = refs[13:]
    place_weights(pos, wo, wx, wgu, wd)
    slot = (lax.broadcasted_iota(jnp.int32, (ROWS, 128), 0) // TILE).astype(F32)
    for k in (0, 1, 2, 3):
        b = lax.div(mod4(pos[0] - k), 2)
        row = pl.multiple_of(b * ROWS, 128)
        tile = cnt[k * 16 : k * 16 + 16, :].astype(F32)
        first = tile[0:1, :]
        last = first + tile[8:9, :]
        mask[0, pl.ds(row, ROWS), :] = jnp.where(slot < first, 1.0, 0.0)
        mask[1, pl.ds(row, ROWS), :] = jnp.where((slot >= first) & (slot < last), 1.0, 0.0)

    @pl.loop(0, 3)
    def _(r):
        at = pl.multiple_of(r * 256, 256)
        rows = pl.ds(at, 256)
        pre = dot(x[rows, :], wgu[...], ((1,), (0,)))
        ma, mb = mask[0, rows, :], mask[1, rows, :]
        is_a = jnp.concatenate([ma, ma], axis=1) > 0.5
        is_b = jnp.concatenate([mb, mb], axis=1) > 0.5
        gate = jnp.where(is_a, pre[:, 0:256], pre[:, 512:768])
        up = jnp.where(is_a, pre[:, 256:512], pre[:, 768:1024])
        gate_out[rows, :] = gate
        up_out[rows, :] = up
        h = gate * jax.nn.sigmoid(gate) * up
        zero = jnp.zeros_like(h)
        hid[rows, 0:256] = jnp.where(is_a, h, zero).astype(BF16)
        hid[rows, 256:512] = jnp.where(is_b, h, zero).astype(BF16)
        for xs in range(4):
            part[xs, rows, :] = dot(
                hid[rows, :], wd[:, xs * 512 : (xs + 1) * 512], ((1,), (0,))
            ).astype(BF16)


def place_tokens(pos, own, before, after, far_a, far_b, x):
    place_rows(pos, (own, before, after, far_a, far_b), 0, x)


def backward_kernel(*refs):
    pos, sp = refs[0], refs[1:6]
    x, wgu, wd, gate_in, up_in, mask, hid = refs[6:13]
    part, d_own, d_other, s, grad, dots = refs[13:]
    dots[...] = jnp.zeros_like(dots)
    place_rows(pos, sp, ROWS, s)

    @pl.loop(0, 3)
    def _(r):
        at = pl.multiple_of(r * 256, 256)
        rows = pl.ds(at, 256)
        both = dot(s[rows, :], wd[...], ((1,), (1,)))
        ma, mb = mask[0, rows, :], mask[1, rows, :]
        is_a = jnp.concatenate([ma, ma], axis=1) > 0.5
        is_b = jnp.concatenate([mb, mb], axis=1) > 0.5
        hg = jnp.where(is_a, both[:, 0:256], both[:, 256:512])
        gate, up = gate_in[rows, :], up_in[rows, :]
        sig = jax.nn.sigmoid(gate)
        pg = hg * up * sig * (1.0 + gate * (1.0 - sig))
        pu = hg * (gate * sig)
        zero = jnp.zeros_like(pg)
        prod = hg * (hid[rows, 0:256].astype(F32) + hid[rows, 256:512].astype(F32))
        sums = lax.dot_general(
            jnp.ones((8, 256), F32),
            prod,
            (((1,), (1,)), ((), ())),
            precision=lax.Precision.HIGHEST,
            preferred_element_type=F32,
        )
        for i in range(2):
            dots[pl.ds(r * 2 + i, 1), :] = sums[0:1, i * 128 : (i + 1) * 128]
        grad[rows, 0:256] = jnp.where(is_a, pg, zero).astype(BF16)
        grad[rows, 256:512] = jnp.where(is_a, pu, zero).astype(BF16)
        grad[rows, 512:768] = jnp.where(is_b, pg, zero).astype(BF16)
        grad[rows, 768:1024] = jnp.where(is_b, pu, zero).astype(BF16)
        for xs in range(4):
            part[xs, rows, :] = dot(
                grad[rows, :], wgu[xs * 512 : (xs + 1) * 512, :], ((1,), (1,))
            ).astype(BF16)

    tile = dots[...].astype(BF16)
    for xs in range(4):
        for i in range(4):
            part[xs, 768:784, i * 128 : (i + 1) * 128] = tile

    dests = (d_own, d_other)

    @pl.loop(0, 4)
    def _(z):
        cols = pl.ds(pl.multiple_of(z * 512, 512), 512)
        dgu = dot(x[:, cols], grad[...], ((0,), (0,))).astype(BF16)
        dd = dot(hid[...], s[:, cols], ((0,), (0,))).astype(BF16)
        for cs in range(2):
            for y in range(4):
                yk, zk = mod4(y - pos[1]), mod4(z - pos[0])
                for e in range(2):
                    for m in range(2):
                        col = (e * 4 + m * 2 + cs) * 128
                        dests[cs][yk, zk, e * 3 + m] = dgu[
                            y * 128 : (y + 1) * 128, col : col + 128
                        ]
                    row = (e * 2 + cs) * 128
                    dests[cs][yk, zk, e * 3 + 2] = dd[
                        row : row + 128, y * 128 : (y + 1) * 128
                    ]


def sum_x_kernel(pos, got, keep, send):
    zl = pos[3]
    for out, at in ((send, (1 - zl) * 256), (keep, zl * 256)):
        cols = pl.ds(pl.multiple_of(at, 128), 256)
        total = got[0, :, cols].astype(F32)
        for i in (1, 2, 3):
            total = total + got[i, :, cols].astype(F32)
        out[...] = total.astype(out.dtype)


def split_kernel(pos, keep, got, o0, o1, o2, o3, tmp):
    tmp[...] = keep[...] + got[...].astype(F32)
    for k, out in enumerate((o0, o1, o2, o3)):
        s = mod4(pos[0] - k)
        row = pl.multiple_of(lax.div(s, 2) * ROWS, 128)
        col = pl.multiple_of(lax.rem(s, 2) * 128, 128)
        out[0:ROWS] = tmp[pl.ds(row, ROWS), pl.ds(col, 128)].astype(BF16)
        if out.shape[0] > ROWS:
            out[ROWS:] = tmp[2 * ROWS :, pl.ds(col, 128)].astype(BF16)


def finish_kernel(pos, p0, p1, p2, p3, gate, up, down):
    for k, ref in enumerate((p0, p1, p2, p3)):
        q = pl.multiple_of(mod4(pos[0] - k) * 128, 128)
        for e in range(2):
            gate[e, :, pl.ds(q, 128)] = ref[e * 3]
            up[e, :, pl.ds(q, 128)] = ref[e * 3 + 1]
            down[e, pl.ds(q, 128), :] = ref[e * 3 + 2]


def add_cores_kernel(a, b, o0, o1, o2, o3):
    for k, out in enumerate((o0, o1, o2, o3)):
        out[...] = (a[k].astype(F32) + b[k].astype(F32)).astype(BF16)


def sum_y_kernel(a, b, c, d, o0, o1, o2, o3):
    for k, out in enumerate((o0, o1, o2, o3)):
        total = a[k].astype(F32) + b[k].astype(F32) + c[k].astype(F32) + d[k].astype(F32)
        out[...] = total.astype(BF16)


def exchange(parts, axis):
    return [parts[0]] + [shift(parts[k], axis, k) for k in (1, 2, 3)]


def scatter_rows(pos, part, deps=(), split_deps=()):
    rows = part.shape[1]
    extra = rows - 2 * ROWS
    keep, send = call(
        sum_x_kernel,
        [((rows, 256), F32), ((rows, 256), BF16)],
        1,
        [pos, lax.all_to_all(part, "x", 0, 0)],
        deps=deps,
    )
    blocks = call(
        split_kernel,
        [((ROWS + extra, 128), BF16)] * 4,
        1,
        [pos, keep, shift(send, "zl", 1)],
        [pltpu.VMEM((rows, 256), F32)],
        deps=split_deps,
    )
    terms = [from_core(b, k).astype(F32) for k, b in enumerate(blocks)]
    return terms[0] + terms[1] + terms[2] + terms[3]


def add_cores(d_own, d_other):
    return call(
        add_cores_kernel,
        [((4, 6, 128, 128), BF16)] * 4,
        0,
        [d_own, shift(d_other, "c", 1)],
    )


def per_device(tokens, cotangent, route_probs, w_gate, w_up, w_down, tile_counts):
    pos = jnp.stack([lax.axis_index(a) for a in SIZES]).astype(jnp.int32)
    (msg,) = call(
        pack_tokens,
        [((2 * ROWS + 16, 128), BF16)],
        1,
        [tile_counts, tokens, cotangent, route_probs[:, None]],
    )
    got = [to_core(msg, k) for k in range(4)]
    cnt = jnp.concatenate([g[2 * ROWS :] for g in got])
    ts = jnp.concatenate(got)
    ts_ring = ring(jnp.concatenate([ts, shift(ts, "zl", 1)]), "x")
    w = call(
        pack_weights,
        [((6, 128, 128), BF16)] * 4,
        1,
        [pos, w_gate, w_up, w_down],
    )
    own = ring(jnp.stack(exchange(w, "zh")), "y")
    other = [shift(v, "c", 1) for v in own]
    (x,) = call(place_tokens, [((768, 2048), BF16)], 1, [pos, *ts_ring])

    wgu, wd, gate, up, mask, hid, part_out = call(
        forward_kernel,
        [
            ((2048, 1024), BF16),
            ((512, 2048), BF16),
            ((768, 256), F32),
            ((768, 256), F32),
            ((2, 768, 128), F32),
            ((768, 512), BF16),
            ((4, 768, 512), BF16),
        ],
        1,
        [pos, cnt, x, *own, *other],
        flops=2 * 768 * 2048 * 1536,
        nbytes=30 << 20,
    )
    part_in, d_own, d_other = call(
        backward_kernel,
        [((4, 784, 512), BF16)] + [((4, 4, 6, 128, 128), BF16)] * 2,
        1,
        [pos, *ts_ring, x, wgu, wd, gate, up, mask, hid],
        [
            pltpu.VMEM((768, 2048), BF16),
            pltpu.VMEM((768, 1024), BF16),
            pltpu.VMEM((16, 128), F32),
        ],
        flops=2 * 768 * 2048 * 3072,
        nbytes=30 << 20,
    )
    four = add_cores(d_own, d_other)
    ffn_out = scatter_rows(pos, part_out, deps=four[:1])
    layer_out = (route_probs[:, None] * ffn_out).astype(BF16)
    four = call(sum_y_kernel, [((6, 128, 128), BF16)] * 4, 0, exchange(four, "y"))
    back = scatter_rows(pos, part_in, deps=[layer_out], split_deps=four[:1])
    gate_grad, up_grad, down_grad = call(
        finish_kernel,
        [((2, 128, 512), BF16), ((2, 128, 512), BF16), ((2, 512, 128), BF16)],
        1,
        [pos, *exchange(four, "zh")],
    )
    input_grad = back[:ROWS].astype(BF16)
    row = ROWS + 3 * lax.rem(lax.axis_index("zh"), 2)
    prob_grad = lax.dynamic_slice_in_dim(back, row, 3, 0).reshape(ROWS) / route_probs
    return layer_out, prob_grad, input_grad, gate_grad, up_grad, down_grad


def solution(mesh):
    fine = Mesh(mesh.devices.reshape(4, 4, 4, 2, 2), tuple(SIZES))
    dp, shard = ("zh", "y"), ("x", "zl", "c")
    rows, cols, both = P(dp, shard), P(None, dp, shard), P(None, shard, dp)
    return jax.shard_map(
        per_device,
        mesh=fine,
        in_specs=(rows, rows, P(dp), cols, cols, both, P(dp, None)),
        out_specs=(rows, P(dp), rows, cols, cols, both),
        check_vma=False,
    )
```

profile of v0, /device:TPU:91, one launch (start us, length us, event | category | flops | bytes accessed | tf_op | source)
XLA Modules:
  0.0 277.7 jit_solution(10604756706159730666)
XLA Ops:
  0.6 1.5 broadcast_in_dim.5.refs_3_
  2.1 1.8 pack_tokens.1
  3.9 6.7 %collective-permute-start.3 = (bf16[784,128]{1,0:T(8,128)(2,1)}, bf16[784,128]{1,0:T(8,128)(2,1)S(1)}, u32[]{:S(2)}, u32[]{:S(2)}) collective-permute-start(bf16[784,128]{1,0:T(8,128)(2,1)} %pack_tokens.1), channel_id=1, source_target_pairs={{0,192},{1,0},{64,64},{65,128},{128,193},{129,1},{192,65},{193,129... | collective-permute-start | bytes 602120 | tf_op jit(solution)/shard_map/ppermute | solution.py:50
  10.7 5.2 %collective-permute-start.1 = (bf16[784,128]{1,0:T(8,128)(2,1)}, bf16[784,128]{1,0:T(8,128)(2,1)S(1)}, u32[]{:S(2)}, u32[]{:S(2)}) collective-permute-start(bf16[784,128]{1,0:T(8,128)(2,1)} %pack_tokens.1), channel_id=1, source_target_pairs={{0,64},{1,128},{64,192},{65,0},{128,65},{129,129},{192,193},{193,1... | collective-permute-start | bytes 602120 | tf_op jit(solution)/shard_map/ppermute | solution.py:50
  15.9 4.4 %collective-permute-start = (bf16[784,128]{1,0:T(8,128)(2,1)}, bf16[784,128]{1,0:T(8,128)(2,1)S(1)}, u32[]{:S(2)}, u32[]{:S(2)}) collective-permute-start(bf16[784,128]{1,0:T(8,128)(2,1)} %pack_tokens.1), channel_id=1, source_target_pairs={{0,0},{1,64},{64,128},{65,192},{128,1},{129,65},{192,129},{193,193... | collective-permute-start | bytes 602120 | tf_op jit(solution)/shard_map/ppermute | solution.py:50
  20.3 2.8 %collective-permute-done.2 = bf16[784,128]{1,0:T(8,128)(2,1)S(1)} collective-permute-done((bf16[784,128]{1,0:T(8,128)(2,1)}, bf16[784,128]{1,0:T(8,128)(2,1)S(1)}, u32[]{:S(2)}, u32[]{:S(2)}) %collective-permute-start.2) | collective-permute-done | bytes 200736 | tf_op jit(solution)/shard_map/ppermute | solution.py:50
  23.1 7.7 %collective-permute-done.1 = bf16[784,128]{1,0:T(8,128)(2,1)S(1)} collective-permute-done((bf16[784,128]{1,0:T(8,128)(2,1)}, bf16[784,128]{1,0:T(8,128)(2,1)S(1)}, u32[]{:S(2)}, u32[]{:S(2)}) %collective-permute-start.1) | collective-permute-done | bytes 200736 | tf_op jit(solution)/shard_map/ppermute | solution.py:50
  30.8 0.9 collective-permute-done
  34.6 15.2 %collective-permute-done.4 = bf16[3136,128]{1,0:T(8,128)(2,1)S(1)} collective-permute-done((bf16[3136,128]{1,0:T(8,128)(2,1)S(1)}, bf16[3136,128]{1,0:T(8,128)(2,1)S(1)}, u32[]{:S(2)}, u32[]{:S(2)}) %collective-permute-start.4) | collective-permute-done | bytes 802848 | tf_op jit(solution)/shard_map/ppermute | solution.py:41
  49.9 0.9 constant_dynamic-update-slice_fusion.refs_1_
  50.8 1.2 collective-permute-start.5
  52.9 2.2 pack_weights.1
  55.1 2.2 collective-permute-start.11
  57.2 3.3 %collective-permute-start.9 = (bf16[6,128,128]{2,1,0:T(8,128)(2,1)}, bf16[6,128,128]{2,1,0:T(8,128)(2,1)S(1)}, u32[]{:S(2)}, u32[]{:S(2)}) collective-permute-start(bf16[6,128,128]{2,1,0:T(8,128)(2,1)} %get-tuple-element.44), channel_id=1, source_target_pairs={{0,64},{64,128},{128,192},{192,0},{1,65},{65,129},{129,193},{193,1... | collective-permute-start | bytes 589832 | tf_op jit(solution)/shard_map/ppermute | solution.py:41
  60.5 13.4 %collective-permute-done.11 = bf16[6,128,128]{2,1,0:T(8,128)(2,1)S(1)} collective-permute-done((bf16[6,128,128]{2,1,0:T(8,128)(2,1)}, bf16[6,128,128]{2,1,0:T(8,128)(2,1)S(1)}, u32[]{:S(2)}, u32[]{:S(2)}) %collective-permute-start.11) | collective-permute-done | bytes 196640 | tf_op jit(solution)/shard_map/ppermute | solution.py:41
  74.0 2.0 collective-permute-done.9
  76.0 1.0 pad_maximum_fusion.1.refs_3_
  77.1 1.5 collective-permute-start.13
  78.6 6.9 %collective-permute-done.5.refs_2_ = bf16[6272,128]{1,0:T(8,128)(2,1)S(1)} collective-permute-done((bf16[6272,128]{1,0:T(8,128)(2,1)}, bf16[6272,128]{1,0:T(8,128)(2,1)S(1)}, u32[]{:S(2)}, u32[]{:S(2)}) %collective-permute-start.5) | collective-permute-done | bytes 1605664 | tf_op jit(solution)/shard_map/ppermute | solution.py:41
  85.6 1.3 collective-permute-start.7
  86.9 1.2 collective-permute-start.8
  88.1 4.8 %collective-permute-done.12.refs_4_ = bf16[4,6,128,128]{3,2,1,0:T(8,128)(2,1)} collective-permute-done((bf16[4,6,128,128]{3,2,1,0:T(8,128)(2,1)S(1)}, bf16[4,6,128,128]{3,2,1,0:T(8,128)(2,1)}, u32[]{:S(2)}, u32[]{:S(2)}) %collective-permute-start.12) | collective-permute-done | bytes 786464 | tf_op jit(solution)/shard_map/ppermute | solution.py:41
  92.9 1.0 slice.43
  93.9 1.4 collective-permute-start.14
  95.3 1.0 slice.44
  96.6 4.8 %collective-permute-start.16 = (bf16[4,6,128,128]{3,2,1,0:T(8,128)(2,1)S(1)}, bf16[4,6,128,128]{3,2,1,0:T(8,128)(2,1)S(1)}, u32[]{:S(2)}, u32[]{:S(2)}) collective-permute-start(bf16[4,6,128,128]{3,2,1,0:T(8,128)(2,1)S(1)} %pad_maximum_fusion.1.refs_3_), channel_id=1, source_target_pairs={{0,1},{1,0},{2,3},{3,2},{4,5},{5,4},{6,7},{7,6},{8,9},{9,8},{10,11... | collective-permute-start | bytes 2359304 | tf_op jit(solution)/shard_map/ppermute | solution.py:41
  101.4 4.7 %collective-permute-start.17 = (bf16[4,6,128,128]{3,2,1,0:T(8,128)(2,1)}, bf16[4,6,128,128]{3,2,1,0:T(8,128)(2,1)S(1)}, u32[]{:S(2)}, u32[]{:S(2)}) collective-permute-start(bf16[4,6,128,128]{3,2,1,0:T(8,128)(2,1)} %collective-permute-done.12.refs_4_), channel_id=1, source_target_pairs={{0,1},{1,0},{2,3},{3,2},{4,5},{5,4},{6,7},{7,6},{8,9},{9,8},{10,11... | collective-permute-start | bytes 2359304 | tf_op jit(solution)/shard_map/ppermute | solution.py:41
  106.1 3.8 %collective-permute-start.18 = (bf16[4,6,128,128]{3,2,1,0:T(8,128)(2,1)}, bf16[4,6,128,128]{3,2,1,0:T(8,128)(2,1)}, u32[]{:S(2)}, u32[]{:S(2)}) collective-permute-start(bf16[4,6,128,128]{3,2,1,0:T(8,128)(2,1)} %collective-permute-done.13.refs_5_), channel_id=1, source_target_pairs={{0,1},{1,0},{2,3},{3,2},{4,5},{5,4},{6,7},{7,6},{8,9},{9,8},{10,11... | collective-permute-start | bytes 2359304 | tf_op jit(solution)/shard_map/ppermute | solution.py:41
  111.1 5.5 %place_tokens.1.refs_2_.refs_6_ = bf16[768,2048]{1,0:T(8,128)(2,1)} custom-call(s32[5]{0:T(128)} %stack.38.refs_0_, bf16[6272,128]{1,0:T(8,128)(2,1)} %constant_dynamic-update-slice_fusion.refs_1_, bf16[6272,128]{1,0:T(8,128)(2,1)} %copy-done.2, bf16[6272,128]{1,0:T(8,128)(2,1)} %copy-done.3, bf16[3136,128]{1,0:T(8,128)(2,1)} %copy-done.7, ...), custom_call_target="tpu_custom_call" | custom-call | tf_op jit(solution)/shard_map/place_tokens/pallas_call | solution.py:23
  116.7 0.8 copy-done.16
  117.9 0.8 copy-done.19
  118.6 14.6 %forward_kernel.1 = (bf16[2048,1024]{1,0:T(8,128)(2,1)}, bf16[512,2048]{1,0:T(8,128)(2,1)}, f32[768,256]{1,0:T(8,128)}, f32[768,256]{1,0:T(8,128)}, f32[2,768,12...) custom-call(s32[5]{0:T(128)} %stack.38.refs_0_, bf16[64,128]{1,0:T(8,128)(2,1)} %pad_maximum_fusion.2.refs_1_, ...), custom_call_target="tpu_custom_call" | custom-call | flops 4831838208 | bytes 31457280 | tf_op jit(solution)/shard_map/forward_kernel/pallas_call | solution.py:23
  133.2 5.1 %all-to-all-start = ((bf16[4,768,512]{2,1,0:T(8,128)(2,1)}), bf16[4,768,512]{2,1,0:T(8,128)(2,1)S(1)}, u32[]{:S(2)}, u32[]{:S(2)}) async-start(bf16[4,768,512]{2,1,0:T(8,128)(2,1)} %get-tuple-element.47), calls=%async_computation | async-start | bytes 6291456 | tf_op jit(solution)/shard_map/all_to_all | solution.py:301
  138.4 23.0 %backward_kernel.1 = (bf16[4,784,512]{2,1,0:T(8,128)(2,1)}, bf16[4,4,6,128,128]{4,3,2,1,0:T(8,128)(2,1)}, bf16[4,4,6,128,128]{4,3,2,1,0:T(8,128)(2,1)}) custom-call(s32[5]{0:T(128)} %stack.38.refs_0_, bf16[6272,128]{1,0:T(8,128)(2,1)} %constant_dynamic-update-slice_fusion.refs_1_, bf16[6272,128]{1,0:T(8,128)(2,1)} %copy-done.2, bf16[6272,128]{1,0:T(8,128)(2,1)} %copy-done.3, ...), custom_call_target="tpu_custom_call" | custom-call | flops 9663676416 | bytes 31457280 | tf_op jit(solution)/shard_map/backward_kernel/pallas_call | solution.py:23
  161.9 12.8 %all-to-all-done.refs_1_ = bf16[4,768,512]{2,1,0:T(8,128)(2,1)S(1)} async-done(((bf16[4,768,512]{2,1,0:T(8,128)(2,1)}), bf16[4,768,512]{2,1,0:T(8,128)(2,1)S(1)}, u32[]{:S(2)}, u32[]{:S(2)}) %all-to-all-start) | async-done | bytes 3145760 | tf_op jit(solution)/shard_map/all_to_all | solution.py:301
  174.7 1.6 copy-done.1
  176.3 4.9 %all-to-all-start.1 = ((bf16[4,784,512]{2,1,0:T(8,128)(2,1)}), bf16[4,784,512]{2,1,0:T(8,128)(2,1)S(1)}, u32[]{:S(2)}, u32[]{:S(2)}) async-start(bf16[4,784,512]{2,1,0:T(8,128)(2,1)} %get-tuple-element.63), calls=%async_computation.1 | async-start | bytes 6422528 | tf_op jit(solution)/shard_map/all_to_all | solution.py:301
  181.2 4.8 %add_cores_kernel.1 = (bf16[4,6,128,128]{3,2,1,0:T(8,128)(2,1)}, bf16[4,6,128,128]{3,2,1,0:T(8,128)(2,1)}, bf16[4,6,128,128]{3,2,1,0:T(8,128)(2,1)}, bf16[4,6,128,128]{3,2,1,0:T(8,128)(2,1)}) custom-call(bf16[4,4,6,128,128]{4,3,2,1,0:T(8,128)(2,1)} %get-tuple-element.54.refs_0_, bf16[4,4,6,128,128]{4,3,2,1,0:T(8,128)(2,1)} %collective-permute-done.21.refs_1_), custom_call_target="tpu_custom_call" | custom-call | tf_op jit(solution)/shard_map/add_cores_kernel/pallas_call | solution.py:23
  186.0 3.2 %sum_x_kernel.2 = (f32[768,256]{1,0:T(8,128)}, bf16[768,256]{1,0:T(8,128)(2,1)}) custom-call(s32[5]{0:T(128)} %stack.38.refs_0_, bf16[4,768,512]{2,1,0:T(8,128)(2,1)} %copy-done.1, bf16[4,6,128,128]{3,2,1,0:T(8,128)(2,1)} %get-tuple-element.56.refs_2_.refs_0_), custom_call_target="tpu_custom_call" | custom-call | tf_op jit(solution)/shard_map/sum_x_kernel/pallas_call | solution.py:23
  189.2 0.8 collective-permute-start.29
  190.7 8.1 %collective-permute-done.22.refs_2_ = bf16[768,256]{1,0:T(8,128)(2,1)S(1)} collective-permute-done((bf16[768,256]{1,0:T(8,128)(2,1)}, bf16[768,256]{1,0:T(8,128)(2,1)S(1)}, u32[]{:S(2)}, u32[]{:S(2)}) %collective-permute-start.22) | collective-permute-done | bytes 393248 | tf_op jit(solution)/shard_map/ppermute | solution.py:41
  198.8 0.8 copy-done.11
  199.6 2.1 split_kernel.2
  201.7 9.7 %collective-permute-start.26 = (bf16[384,128]{1,0:T(8,128)(2,1)}, bf16[384,128]{1,0:T(8,128)(2,1)S(1)}, u32[]{:S(2)}, u32[]{:S(2)}) collective-permute-start(bf16[384,128]{1,0:T(8,128)(2,1)} %get-tuple-element.62), channel_id=1, source_target_pairs={{192,0},{0,1},{64,64},{128,65},{193,128},{1,129},{65,192},{129,193... | collective-permute-start | bytes 294920 | tf_op jit(solution)/shard_map/ppermute | solution.py:59
  211.4 1.8 collective-permute-done.26
  213.3 1.9 collective-permute-start.24
  215.2 3.3 %collective-permute-start.23 = (bf16[384,128]{1,0:T(8,128)(2,1)}, bf16[384,128]{1,0:T(8,128)(2,1)S(1)}, u32[]{:S(2)}, u32[]{:S(2)}) collective-permute-start(bf16[384,128]{1,0:T(8,128)(2,1)} %get-tuple-element.59), channel_id=1, source_target_pairs={{0,0},{64,1},{128,64},{192,65},{1,128},{65,129},{129,192},{193,193... | collective-permute-start | bytes 294920 | tf_op jit(solution)/shard_map/ppermute | solution.py:59
  218.6 2.9 %collective-permute-done.24 = bf16[384,128]{1,0:T(8,128)(2,1)S(1)} collective-permute-done((bf16[384,128]{1,0:T(8,128)(2,1)}, bf16[384,128]{1,0:T(8,128)(2,1)S(1)}, u32[]{:S(2)}, u32[]{:S(2)}) %collective-permute-start.24) | collective-permute-done | bytes 98336 | tf_op jit(solution)/shard_map/ppermute | solution.py:59
  221.5 4.4 %collective-permute-done.23 = bf16[384,128]{1,0:T(8,128)(2,1)S(1)} collective-permute-done((bf16[384,128]{1,0:T(8,128)(2,1)}, bf16[384,128]{1,0:T(8,128)(2,1)S(1)}, u32[]{:S(2)}, u32[]{:S(2)}) %collective-permute-start.23) | collective-permute-done | bytes 98336 | tf_op jit(solution)/shard_map/ppermute | solution.py:59
  225.9 0.8 multiply_convert_fusion.refs_2_
  226.7 1.7 copy-done
  228.4 3.3 %sum_x_kernel.3 = (f32[784,256]{1,0:T(8,128)}, bf16[784,256]{1,0:T(8,128)(2,1)}) custom-call(s32[5]{0:T(128)} %stack.38.refs_0_, bf16[4,784,512]{2,1,0:T(8,128)(2,1)} %copy-done, bf16[384,128]{1,0:T(8,128)(2,1)} %multiply_convert_fusion.refs_2_), custom_call_target="tpu_custom_call" | custom-call | tf_op jit(solution)/shard_map/sum_x_kernel/pallas_call | solution.py:23
  231.6 2.6 collective-permute-start.27
  234.3 2.9 %sum_y_kernel.1 = (bf16[6,128,128]{2,1,0:T(8,128)(2,1)}, bf16[6,128,128]{2,1,0:T(8,128)(2,1)}, bf16[6,128,128]{2,1,0:T(8,128)(2,1)}, bf16[6,128,128]{2,1,0:T(8,128)(2,1)}) custom-call(bf16[4,6,128,128]{3,2,1,0:T(8,128)(2,1)} %get-tuple-element.56.refs_2_.refs_0_, bf16[4,6,128,128]{3,2,1,0:T(8,128)(2,1)} %collective-permute-done.28.refs_1_, ...), custom_call_target="tpu_custom_call" | custom-call | tf_op jit(solution)/shard_map/sum_y_kernel/pallas_call | solution.py:23
  237.2 2.4 collective-permute-start.36
  239.8 6.3 %collective-permute-done.27.refs_2_ = bf16[784,256]{1,0:T(8,128)(2,1)S(1)} collective-permute-done((bf16[784,256]{1,0:T(8,128)(2,1)}, bf16[784,256]{1,0:T(8,128)(2,1)S(1)}, u32[]{:S(2)}, u32[]{:S(2)}) %collective-permute-start.27) | collective-permute-done | bytes 401440 | tf_op jit(solution)/shard_map/ppermute | solution.py:41
  246.1 0.8 copy-done.10
  246.9 2.1 split_kernel.3
  249.0 5.3 %collective-permute-start.34 = (bf16[400,128]{1,0:T(8,128)(2,1)}, bf16[400,128]{1,0:T(8,128)(2,1)S(1)}, u32[]{:S(2)}, u32[]{:S(2)}) collective-permute-start(bf16[400,128]{1,0:T(8,128)(2,1)} %get-tuple-element.73), channel_id=1, source_target_pairs={{192,0},{0,1},{64,64},{128,65},{193,128},{1,129},{65,192},{129,193... | collective-permute-start | bytes 307208 | tf_op jit(solution)/shard_map/ppermute | solution.py:59
  254.4 3.2 %collective-permute-start.33 = (bf16[400,128]{1,0:T(8,128)(2,1)}, bf16[400,128]{1,0:T(8,128)(2,1)S(1)}, u32[]{:S(2)}, u32[]{:S(2)}) collective-permute-start(bf16[400,128]{1,0:T(8,128)(2,1)} %get-tuple-element.72), channel_id=1, source_target_pairs={{128,0},{192,1},{0,64},{64,65},{129,128},{193,129},{1,192},{65,193... | collective-permute-start | bytes 307208 | tf_op jit(solution)/shard_map/ppermute | solution.py:59
  257.5 7.9 %collective-permute-start.32 = (bf16[400,128]{1,0:T(8,128)(2,1)}, bf16[400,128]{1,0:T(8,128)(2,1)S(1)}, u32[]{:S(2)}, u32[]{:S(2)}) collective-permute-start(bf16[400,128]{1,0:T(8,128)(2,1)} %get-tuple-element.71), channel_id=1, source_target_pairs={{64,0},{128,1},{192,64},{0,65},{65,128},{129,129},{193,192},{1,193... | collective-permute-start | bytes 307208 | tf_op jit(solution)/shard_map/ppermute | solution.py:59
  265.5 1.9 collective-permute-start.31
  268.1 2.2 finish_kernel.1
  270.4 6.1 %collective-permute-done.31 = bf16[400,128]{1,0:T(8,128)(2,1)S(1)} collective-permute-done((bf16[400,128]{1,0:T(8,128)(2,1)}, bf16[400,128]{1,0:T(8,128)(2,1)S(1)}, u32[]{:S(2)}, u32[]{:S(2)}) %collective-permute-start.31) | collective-permute-done | bytes 102432 | tf_op jit(solution)/shard_map/ppermute | solution.py:59
  (93 shorter events, 9.4 us)
Async XLA Ops:
  3.9 16.3 %collective-permute-start.3 = (bf16[784,128]{1,0:T(8,128)(2,1)}, bf16[784,128]{1,0:T(8,128)(2,1)S(1)}, u32[]{:S(2)}, u32[]{:S(2)}) collective-permute-start(bf16[784,128]{1,0:T(8,128)(2,1)} %pack_tokens.1), channel_id=1, source_target_pairs={{0,192},{1,0},{64,64},{65,128},{128,193},{129,1},{192,65},{193,129... | collective-permute-start | bytes 602120 | tf_op jit(solution)/shard_map/ppermute | solution.py:50
  10.6 12.5 %collective-permute-start.2 = (bf16[784,128]{1,0:T(8,128)(2,1)}, bf16[784,128]{1,0:T(8,128)(2,1)S(1)}, u32[]{:S(2)}, u32[]{:S(2)}) collective-permute-start(bf16[784,128]{1,0:T(8,128)(2,1)} %pack_tokens.1), channel_id=1, source_target_pairs={{0,128},{1,192},{64,0},{65,64},{128,129},{129,193},{192,1},{193,65... | collective-permute-start | bytes 602120 | tf_op jit(solution)/shard_map/ppermute | solution.py:50
  10.7 20.1 %collective-permute-start.1 = (bf16[784,128]{1,0:T(8,128)(2,1)}, bf16[784,128]{1,0:T(8,128)(2,1)S(1)}, u32[]{:S(2)}, u32[]{:S(2)}) collective-permute-start(bf16[784,128]{1,0:T(8,128)(2,1)} %pack_tokens.1), channel_id=1, source_target_pairs={{0,64},{1,128},{64,192},{65,0},{128,65},{129,129},{192,193},{193,1... | collective-permute-start | bytes 602120 | tf_op jit(solution)/shard_map/ppermute | solution.py:50
  15.9 15.8 %collective-permute-start = (bf16[784,128]{1,0:T(8,128)(2,1)}, bf16[784,128]{1,0:T(8,128)(2,1)S(1)}, u32[]{:S(2)}, u32[]{:S(2)}) collective-permute-start(bf16[784,128]{1,0:T(8,128)(2,1)} %pack_tokens.1), channel_id=1, source_target_pairs={{0,0},{1,64},{64,128},{65,192},{128,1},{129,65},{192,129},{193,193... | collective-permute-start | bytes 602120 | tf_op jit(solution)/shard_map/ppermute | solution.py:50
  23.1 11.5 %copy-start.4 = (bf16[784,128]{1,0:T(8,128)(2,1)}, bf16[784,128]{1,0:T(8,128)(2,1)S(1)}, u32[]{:S(2)}) copy-start(bf16[784,128]{1,0:T(8,128)(2,1)S(1)} %collective-permute-done.2) | copy-start | bytes 602116
  30.8 3.8 %copy-start.5 = (bf16[784,128]{1,0:T(8,128)(2,1)}, bf16[784,128]{1,0:T(8,128)(2,1)S(1)}, u32[]{:S(2)}) copy-start(bf16[784,128]{1,0:T(8,128)(2,1)S(1)} %collective-permute-done.1) | copy-start | bytes 602116
  31.7 3.0 %copy-start.6 = (bf16[784,128]{1,0:T(8,128)(2,1)}, bf16[784,128]{1,0:T(8,128)(2,1)S(1)}, u32[]{:S(2)}) copy-start(bf16[784,128]{1,0:T(8,128)(2,1)S(1)} %collective-permute-done) | copy-start | bytes 602116
  31.8 18.1 %collective-permute-start.4 = (bf16[3136,128]{1,0:T(8,128)(2,1)S(1)}, bf16[3136,128]{1,0:T(8,128)(2,1)S(1)}, u32[]{:S(2)}, u32[]{:S(2)}) collective-permute-start(bf16[3136,128]{1,0:T(8,128)(2,1)S(1)} %pad_maximum_fusion), channel_id=1, source_target_pairs={{0,2},{2,0},{1,3},{3,1},{4,6},{6,4},{5,7},{7,5},{8,10},{10,8},{9,1... | collective-permute-start | bytes 2408456 | tf_op jit(solution)/shard_map/ppermute | solution.py:41
  50.8 34.6 %collective-permute-start.5 = (bf16[6272,128]{1,0:T(8,128)(2,1)}, bf16[6272,128]{1,0:T(8,128)(2,1)S(1)}, u32[]{:S(2)}, u32[]{:S(2)}) collective-permute-start(bf16[6272,128]{1,0:T(8,128)(2,1)} %constant_dynamic-update-slice_fusion.refs_1_), channel_id=1, source_target_pairs={{0,4},{4,8},{8,12},{12,0},{1,5},{5,9},{9,13},{13,1},{2,6},{6,10},{... | collective-permute-start | bytes 4816904 | tf_op jit(solution)/shard_map/ppermute | solution.py:41
  52.0 34.8 %collective-permute-start.6 = (bf16[6272,128]{1,0:T(8,128)(2,1)}, bf16[6272,128]{1,0:T(8,128)(2,1)S(1)}, u32[]{:S(2)}, u32[]{:S(2)}) collective-permute-start(bf16[6272,128]{1,0:T(8,128)(2,1)} %constant_dynamic-update-slice_fusion.refs_1_), channel_id=1, source_target_pairs={{0,12},{4,0},{8,4},{12,8},{1,13},{5,1},{9,5},{13,9},{2,14},{6,2},{... | collective-permute-start | bytes 4816904 | tf_op jit(solution)/shard_map/ppermute | solution.py:41
  55.1 18.9 %collective-permute-start.11 = (bf16[6,128,128]{2,1,0:T(8,128)(2,1)}, bf16[6,128,128]{2,1,0:T(8,128)(2,1)S(1)}, u32[]{:S(2)}, u32[]{:S(2)}) collective-permute-start(bf16[6,128,128]{2,1,0:T(8,128)(2,1)} %get-tuple-element.46), channel_id=1, source_target_pairs={{0,192},{64,0},{128,64},{192,128},{1,193},{65,1},{129,65},{193,129... | collective-permute-start | bytes 589832 | tf_op jit(solution)/shard_map/ppermute | solution.py:41
  57.2 16.7 %collective-permute-start.10 = (bf16[6,128,128]{2,1,0:T(8,128)(2,1)}, bf16[6,128,128]{2,1,0:T(8,128)(2,1)S(1)}, u32[]{:S(2)}, u32[]{:S(2)}) collective-permute-start(bf16[6,128,128]{2,1,0:T(8,128)(2,1)} %get-tuple-element.45), channel_id=1, source_target_pairs={{0,128},{64,192},{128,0},{192,64},{1,129},{65,193},{129,1},{193,65... | collective-permute-start | bytes 589832 | tf_op jit(solution)/shard_map/ppermute | solution.py:41
  57.2 18.7 %collective-permute-start.9 = (bf16[6,128,128]{2,1,0:T(8,128)(2,1)}, bf16[6,128,128]{2,1,0:T(8,128)(2,1)S(1)}, u32[]{:S(2)}, u32[]{:S(2)}) collective-permute-start(bf16[6,128,128]{2,1,0:T(8,128)(2,1)} %get-tuple-element.44), channel_id=1, source_target_pairs={{0,64},{64,128},{128,192},{192,0},{1,65},{65,129},{129,193},{193,1... | collective-permute-start | bytes 589832 | tf_op jit(solution)/shard_map/ppermute | solution.py:41
  77.0 19.6 %copy-start.9 = (bf16[4,6,128,128]{3,2,1,0:T(8,128)(2,1)}, bf16[4,6,128,128]{3,2,1,0:T(8,128)(2,1)S(1)}, u32[]{:S(2)}) copy-start(bf16[4,6,128,128]{3,2,1,0:T(8,128)(2,1)S(1)} %pad_maximum_fusion.1.refs_3_) | copy-start | bytes 2359300
  77.0 15.9 %collective-permute-start.12 = (bf16[4,6,128,128]{3,2,1,0:T(8,128)(2,1)S(1)}, bf16[4,6,128,128]{3,2,1,0:T(8,128)(2,1)}, u32[]{:S(2)}, u32[]{:S(2)}) collective-permute-start(bf16[4,6,128,128]{3,2,1,0:T(8,128)(2,1)S(1)} %pad_maximum_fusion.1.refs_3_), channel_id=1, source_target_pairs={{0,16},{16,32},{32,48},{48,0},{1,17},{17,33},{33,49},{49,1},{2,18}... | collective-permute-start | bytes 2359304 | tf_op jit(solution)/shard_map/ppermute | solution.py:41
  77.1 18.2 %collective-permute-start.13 = (bf16[4,6,128,128]{3,2,1,0:T(8,128)(2,1)S(1)}, bf16[4,6,128,128]{3,2,1,0:T(8,128)(2,1)}, u32[]{:S(2)}, u32[]{:S(2)}) collective-permute-start(bf16[4,6,128,128]{3,2,1,0:T(8,128)(2,1)S(1)} %pad_maximum_fusion.1.refs_3_), channel_id=1, source_target_pairs={{0,48},{16,0},{32,16},{48,32},{1,49},{17,1},{33,17},{49,33},{2,50}... | collective-permute-start | bytes 2359304 | tf_op jit(solution)/shard_map/ppermute | solution.py:41
  85.5 1.4 copy-start.2
  85.5 25.0 %slice-start = ((bf16[784,128]{1,0:T(8,128)(2,1)}), bf16[16,128]{1,0:T(8,128)(2,1)S(1)}, s32[]{:S(2)}) async-start(bf16[784,128]{1,0:T(8,128)(2,1)} %copy-done.4), calls=%async_computation.2 | async-start | bytes 8192 | tf_op jit(solution)/shard_map/slice | solution.py:334
  85.5 24.9 %slice-start.1 = ((bf16[784,128]{1,0:T(8,128)(2,1)}), bf16[16,128]{1,0:T(8,128)(2,1)S(1)}, s32[]{:S(2)}) async-start(bf16[784,128]{1,0:T(8,128)(2,1)} %copy-done.5), calls=%async_computation.3 | async-start | bytes 8192 | tf_op jit(solution)/shard_map/slice | solution.py:334
  85.6 24.9 %slice-start.2 = ((bf16[784,128]{1,0:T(8,128)(2,1)}), bf16[16,128]{1,0:T(8,128)(2,1)S(1)}, s32[]{:S(2)}) async-start(bf16[784,128]{1,0:T(8,128)(2,1)} %copy-done.6), calls=%async_computation.4 | async-start | bytes 8192 | tf_op jit(solution)/shard_map/slice | solution.py:334
  85.6 24.4 %collective-permute-start.7 = (bf16[3136,128]{1,0:T(8,128)(2,1)S(1)}, bf16[3136,128]{1,0:T(8,128)(2,1)S(1)}, u32[]{:S(2)}, u32[]{:S(2)}) collective-permute-start(bf16[3136,128]{1,0:T(8,128)(2,1)S(1)} %slice.41), channel_id=1, source_target_pairs={{0,4},{4,8},{8,12},{12,0},{1,5},{5,9},{9,13},{13,1},{2,6},{6,10},{... | collective-permute-start | bytes 2408456 | tf_op jit(solution)/shard_map/ppermute | solution.py:41
  86.9 24.3 %copy-start.3 = (bf16[6272,128]{1,0:T(8,128)(2,1)}, bf16[6272,128]{1,0:T(8,128)(2,1)S(1)}, u32[]{:S(2)}) copy-start(bf16[6272,128]{1,0:T(8,128)(2,1)S(1)} %collective-permute-done.6.refs_3_) | copy-start | bytes 4816900
  86.9 23.1 %collective-permute-start.8 = (bf16[3136,128]{1,0:T(8,128)(2,1)S(1)}, bf16[3136,128]{1,0:T(8,128)(2,1)S(1)}, u32[]{:S(2)}, u32[]{:S(2)}) collective-permute-start(bf16[3136,128]{1,0:T(8,128)(2,1)S(1)} %slice.42), channel_id=1, source_target_pairs={{0,12},{4,0},{8,4},{12,8},{1,13},{5,1},{9,5},{13,9},{2,14},{6,2},{... | collective-permute-start | bytes 2408456 | tf_op jit(solution)/shard_map/ppermute | solution.py:41
  93.9 7.5 %collective-permute-start.14 = (bf16[2,6,128,128]{3,2,1,0:T(8,128)(2,1)S(1)}, bf16[2,6,128,128]{3,2,1,0:T(8,128)(2,1)}, u32[]{:S(2)}, u32[]{:S(2)}) collective-permute-start(bf16[2,6,128,128]{3,2,1,0:T(8,128)(2,1)S(1)} %slice.43), channel_id=1, source_target_pairs={{0,16},{16,32},{32,48},{48,0},{1,17},{17,33},{33,49},{49,1},{2,18}... | collective-permute-start | bytes 1179656 | tf_op jit(solution)/shard_map/ppermute | solution.py:41
  96.3 9.8 %collective-permute-start.15 = (bf16[2,6,128,128]{3,2,1,0:T(8,128)(2,1)S(1)}, bf16[2,6,128,128]{3,2,1,0:T(8,128)(2,1)}, u32[]{:S(2)}, u32[]{:S(2)}) collective-permute-start(bf16[2,6,128,128]{3,2,1,0:T(8,128)(2,1)S(1)} %slice.44), channel_id=1, source_target_pairs={{0,48},{16,0},{32,16},{48,32},{1,49},{17,1},{33,17},{49,33},{2,50}... | collective-permute-start | bytes 1179656 | tf_op jit(solution)/shard_map/ppermute | solution.py:41
  96.6 20.0 %collective-permute-start.16 = (bf16[4,6,128,128]{3,2,1,0:T(8,128)(2,1)S(1)}, bf16[4,6,128,128]{3,2,1,0:T(8,128)(2,1)S(1)}, u32[]{:S(2)}, u32[]{:S(2)}) collective-permute-start(bf16[4,6,128,128]{3,2,1,0:T(8,128)(2,1)S(1)} %pad_maximum_fusion.1.refs_3_), channel_id=1, source_target_pairs={{0,1},{1,0},{2,3},{3,2},{4,5},{5,4},{6,7},{7,6},{8,9},{9,8},{10,11... | collective-permute-start | bytes 2359304 | tf_op jit(solution)/shard_map/ppermute | solution.py:41
  101.4 15.2 %collective-permute-start.17 = (bf16[4,6,128,128]{3,2,1,0:T(8,128)(2,1)}, bf16[4,6,128,128]{3,2,1,0:T(8,128)(2,1)S(1)}, u32[]{:S(2)}, u32[]{:S(2)}) collective-permute-start(bf16[4,6,128,128]{3,2,1,0:T(8,128)(2,1)} %collective-permute-done.12.refs_4_), channel_id=1, source_target_pairs={{0,1},{1,0},{2,3},{3,2},{4,5},{5,4},{6,7},{7,6},{8,9},{9,8},{10,11... | collective-permute-start | bytes 2359304 | tf_op jit(solution)/shard_map/ppermute | solution.py:41
  106.1 10.5 %collective-permute-start.18 = (bf16[4,6,128,128]{3,2,1,0:T(8,128)(2,1)}, bf16[4,6,128,128]{3,2,1,0:T(8,128)(2,1)}, u32[]{:S(2)}, u32[]{:S(2)}) collective-permute-start(bf16[4,6,128,128]{3,2,1,0:T(8,128)(2,1)} %collective-permute-done.13.refs_5_), channel_id=1, source_target_pairs={{0,1},{1,0},{2,3},{3,2},{4,5},{5,4},{6,7},{7,6},{8,9},{9,8},{10,11... | collective-permute-start | bytes 2359304 | tf_op jit(solution)/shard_map/ppermute | solution.py:41
  110.0 1.2 copy-start.7
  110.0 6.7 %collective-permute-start.19 = (bf16[2,6,128,128]{3,2,1,0:T(8,128)(2,1)}, bf16[2,6,128,128]{3,2,1,0:T(8,128)(2,1)S(1)}, u32[]{:S(2)}, u32[]{:S(2)}) collective-permute-start(bf16[2,6,128,128]{3,2,1,0:T(8,128)(2,1)} %collective-permute-done.14.refs_6_), channel_id=1, source_target_pairs={{0,1},{1,0},{2,3},{3,2},{4,5},{5,4},{6,7},{7,6},{8,9},{9,8},{10,11... | collective-permute-start | bytes 1179656 | tf_op jit(solution)/shard_map/ppermute | solution.py:41
  110.1 1.1 copy-start.8
  110.1 6.6 %collective-permute-start.20 = (bf16[2,6,128,128]{3,2,1,0:T(8,128)(2,1)}, bf16[2,6,128,128]{3,2,1,0:T(8,128)(2,1)S(1)}, u32[]{:S(2)}, u32[]{:S(2)}) collective-permute-start(bf16[2,6,128,128]{3,2,1,0:T(8,128)(2,1)} %collective-permute-done.15.refs_7_), channel_id=1, source_target_pairs={{0,1},{1,0},{2,3},{3,2},{4,5},{5,4},{6,7},{7,6},{8,9},{9,8},{10,11... | collective-permute-start | bytes 1179656 | tf_op jit(solution)/shard_map/ppermute | solution.py:41
  116.6 0.9 copy-start.16
  116.6 1.2 copy-start.17
  116.6 1.2 copy-start.18
  117.9 0.8 copy-start.19
  133.2 41.4 %all-to-all-start = ((bf16[4,768,512]{2,1,0:T(8,128)(2,1)}), bf16[4,768,512]{2,1,0:T(8,128)(2,1)S(1)}, u32[]{:S(2)}, u32[]{:S(2)}) async-start(bf16[4,768,512]{2,1,0:T(8,128)(2,1)} %get-tuple-element.47), calls=%async_computation | async-start | bytes 6291456 | tf_op jit(solution)/shard_map/all_to_all | solution.py:301
  161.4 19.8 %collective-permute-start.21 = (bf16[4,4,6,128,128]{4,3,2,1,0:T(8,128)(2,1)}, bf16[4,4,6,128,128]{4,3,2,1,0:T(8,128)(2,1)}, u32[]{:S(2)}, u32[]{:S(2)}) collective-permute-start(bf16[4,4,6,128,128]{4,3,2,1,0:T(8,128)(2,1)} %get-tuple-element.55), channel_id=1, source_target_pairs={{0,1},{1,0},{2,3},{3,2},{4,5},{5,4},{6,7},{7,6},{8,9},{9,8},{10,11... | collective-permute-start | bytes 9437192 | tf_op jit(solution)/shard_map/ppermute | solution.py:41
  174.7 1.6 copy-start.1
  176.3 50.4 %all-to-all-start.1 = ((bf16[4,784,512]{2,1,0:T(8,128)(2,1)}), bf16[4,784,512]{2,1,0:T(8,128)(2,1)S(1)}, u32[]{:S(2)}, u32[]{:S(2)}) async-start(bf16[4,784,512]{2,1,0:T(8,128)(2,1)} %get-tuple-element.63), calls=%async_computation.1 | async-start | bytes 6422528 | tf_op jit(solution)/shard_map/all_to_all | solution.py:301
  186.0 40.0 %copy-start.15 = (f32[384]{0:T(512)S(1)}, f32[384]{0:T(512)}, u32[]{:S(2)}) copy-start(f32[384]{0:T(512)} %param.9) | copy-start | bytes 4612
  189.2 9.6 %collective-permute-start.22 = (bf16[768,256]{1,0:T(8,128)(2,1)}, bf16[768,256]{1,0:T(8,128)(2,1)S(1)}, u32[]{:S(2)}, u32[]{:S(2)}) collective-permute-start(bf16[768,256]{1,0:T(8,128)(2,1)} %get-tuple-element.58), channel_id=1, source_target_pairs={{0,2},{2,0},{1,3},{3,1},{4,6},{6,4},{5,7},{7,5},{8,10},{10,8},{9,1... | collective-permute-start | bytes 1179656 | tf_op jit(solution)/shard_map/ppermute | solution.py:41
  189.2 45.1 %collective-permute-start.28 = (bf16[4,6,128,128]{3,2,1,0:T(8,128)(2,1)}, bf16[4,6,128,128]{3,2,1,0:T(8,128)(2,1)}, u32[]{:S(2)}, u32[]{:S(2)}) collective-permute-start(bf16[4,6,128,128]{3,2,1,0:T(8,128)(2,1)} %get-tuple-element.66), channel_id=1, source_target_pairs={{0,16},{16,32},{32,48},{48,0},{1,17},{17,33},{33,49},{49,1},{2,18}... | collective-permute-start | bytes 2359304 | tf_op jit(solution)/shard_map/ppermute | solution.py:41
  189.2 45.1 %collective-permute-start.29 = (bf16[4,6,128,128]{3,2,1,0:T(8,128)(2,1)}, bf16[4,6,128,128]{3,2,1,0:T(8,128)(2,1)}, u32[]{:S(2)}, u32[]{:S(2)}) collective-permute-start(bf16[4,6,128,128]{3,2,1,0:T(8,128)(2,1)} %get-tuple-element.67), channel_id=1, source_target_pairs={{0,32},{16,48},{32,0},{48,16},{1,33},{17,49},{33,1},{49,17},{2,34}... | collective-permute-start | bytes 2359304 | tf_op jit(solution)/shard_map/ppermute | solution.py:41
  190.0 44.3 %collective-permute-start.30 = (bf16[4,6,128,128]{3,2,1,0:T(8,128)(2,1)}, bf16[4,6,128,128]{3,2,1,0:T(8,128)(2,1)}, u32[]{:S(2)}, u32[]{:S(2)}) collective-permute-start(bf16[4,6,128,128]{3,2,1,0:T(8,128)(2,1)} %get-tuple-element.68), channel_id=1, source_target_pairs={{0,48},{16,0},{32,16},{48,32},{1,49},{17,1},{33,17},{49,33},{2,50}... | collective-permute-start | bytes 2359304 | tf_op jit(solution)/shard_map/ppermute | solution.py:41
  198.8 0.8 copy-start.11
  201.7 11.6 %collective-permute-start.26 = (bf16[384,128]{1,0:T(8,128)(2,1)}, bf16[384,128]{1,0:T(8,128)(2,1)S(1)}, u32[]{:S(2)}, u32[]{:S(2)}) collective-permute-start(bf16[384,128]{1,0:T(8,128)(2,1)} %get-tuple-element.62), channel_id=1, source_target_pairs={{192,0},{0,1},{64,64},{128,65},{193,128},{1,129},{65,192},{129,193... | collective-permute-start | bytes 294920 | tf_op jit(solution)/shard_map/ppermute | solution.py:59
  211.3 3.9 %collective-permute-start.25 = (bf16[384,128]{1,0:T(8,128)(2,1)}, bf16[384,128]{1,0:T(8,128)(2,1)S(1)}, u32[]{:S(2)}, u32[]{:S(2)}) collective-permute-start(bf16[384,128]{1,0:T(8,128)(2,1)} %get-tuple-element.61), channel_id=1, source_target_pairs={{128,0},{192,1},{0,64},{64,65},{129,128},{193,129},{1,192},{65,193... | collective-permute-start | bytes 294920 | tf_op jit(solution)/shard_map/ppermute | solution.py:59
  213.3 8.2 %collective-permute-start.24 = (bf16[384,128]{1,0:T(8,128)(2,1)}, bf16[384,128]{1,0:T(8,128)(2,1)S(1)}, u32[]{:S(2)}, u32[]{:S(2)}) collective-permute-start(bf16[384,128]{1,0:T(8,128)(2,1)} %get-tuple-element.60), channel_id=1, source_target_pairs={{64,0},{128,1},{192,64},{0,65},{65,128},{129,129},{193,192},{1,193... | collective-permute-start | bytes 294920 | tf_op jit(solution)/shard_map/ppermute | solution.py:59
  215.2 10.7 %collective-permute-start.23 = (bf16[384,128]{1,0:T(8,128)(2,1)}, bf16[384,128]{1,0:T(8,128)(2,1)S(1)}, u32[]{:S(2)}, u32[]{:S(2)}) collective-permute-start(bf16[384,128]{1,0:T(8,128)(2,1)} %get-tuple-element.59), channel_id=1, source_target_pairs={{0,0},{64,1},{128,64},{192,65},{1,128},{65,129},{129,192},{193,193... | collective-permute-start | bytes 294920 | tf_op jit(solution)/shard_map/ppermute | solution.py:59
  226.7 1.7 copy-start
  231.6 14.5 %collective-permute-start.27 = (bf16[784,256]{1,0:T(8,128)(2,1)}, bf16[784,256]{1,0:T(8,128)(2,1)S(1)}, u32[]{:S(2)}, u32[]{:S(2)}) collective-permute-start(bf16[784,256]{1,0:T(8,128)(2,1)} %get-tuple-element.65), channel_id=1, source_target_pairs={{0,2},{2,0},{1,3},{3,1},{4,6},{6,4},{5,7},{7,5},{8,10},{10,8},{9,1... | collective-permute-start | bytes 1204232 | tf_op jit(solution)/shard_map/ppermute | solution.py:41
  237.2 20.3 %collective-permute-start.35 = (bf16[6,128,128]{2,1,0:T(8,128)(2,1)}, bf16[6,128,128]{2,1,0:T(8,128)(2,1)S(1)}, u32[]{:S(2)}, u32[]{:S(2)}) collective-permute-start(bf16[6,128,128]{2,1,0:T(8,128)(2,1)} %get-tuple-element.74), channel_id=1, source_target_pairs={{0,64},{64,128},{128,192},{192,0},{1,65},{65,129},{129,193},{193,1... | collective-permute-start | bytes 589832 | tf_op jit(solution)/shard_map/ppermute | solution.py:41
  237.2 28.3 %collective-permute-start.36 = (bf16[6,128,128]{2,1,0:T(8,128)(2,1)}, bf16[6,128,128]{2,1,0:T(8,128)(2,1)S(1)}, u32[]{:S(2)}, u32[]{:S(2)}) collective-permute-start(bf16[6,128,128]{2,1,0:T(8,128)(2,1)} %get-tuple-element.75), channel_id=1, source_target_pairs={{0,128},{64,192},{128,0},{192,64},{1,129},{65,193},{129,1},{193,65... | collective-permute-start | bytes 589832 | tf_op jit(solution)/shard_map/ppermute | solution.py:41
  239.6 27.8 %collective-permute-start.37 = (bf16[6,128,128]{2,1,0:T(8,128)(2,1)}, bf16[6,128,128]{2,1,0:T(8,128)(2,1)S(1)}, u32[]{:S(2)}, u32[]{:S(2)}) collective-permute-start(bf16[6,128,128]{2,1,0:T(8,128)(2,1)} %get-tuple-element.76), channel_id=1, source_target_pairs={{0,192},{64,0},{128,64},{192,128},{1,193},{65,1},{129,65},{193,129... | collective-permute-start | bytes 589832 | tf_op jit(solution)/shard_map/ppermute | solution.py:41
  246.1 0.8 copy-start.10
  249.0 21.4 %collective-permute-start.34 = (bf16[400,128]{1,0:T(8,128)(2,1)}, bf16[400,128]{1,0:T(8,128)(2,1)S(1)}, u32[]{:S(2)}, u32[]{:S(2)}) collective-permute-start(bf16[400,128]{1,0:T(8,128)(2,1)} %get-tuple-element.73), channel_id=1, source_target_pairs={{192,0},{0,1},{64,64},{128,65},{193,128},{1,129},{65,192},{129,193... | collective-permute-start | bytes 307208 | tf_op jit(solution)/shard_map/ppermute | solution.py:59
  254.4 16.0 %collective-permute-start.33 = (bf16[400,128]{1,0:T(8,128)(2,1)}, bf16[400,128]{1,0:T(8,128)(2,1)S(1)}, u32[]{:S(2)}, u32[]{:S(2)}) collective-permute-start(bf16[400,128]{1,0:T(8,128)(2,1)} %get-tuple-element.72), channel_id=1, source_target_pairs={{128,0},{192,1},{0,64},{64,65},{129,128},{193,129},{1,192},{65,193... | collective-permute-start | bytes 307208 | tf_op jit(solution)/shard_map/ppermute | solution.py:59
  257.5 9.9 %copy-start.12 = (bf16[6,128,128]{2,1,0:T(8,128)(2,1)}, bf16[6,128,128]{2,1,0:T(8,128)(2,1)S(1)}, u32[]{:S(2)}) copy-start(bf16[6,128,128]{2,1,0:T(8,128)(2,1)S(1)} %collective-permute-done.35.refs_2_) | copy-start | bytes 589828
  257.5 12.8 %collective-permute-start.32 = (bf16[400,128]{1,0:T(8,128)(2,1)}, bf16[400,128]{1,0:T(8,128)(2,1)S(1)}, u32[]{:S(2)}, u32[]{:S(2)}) collective-permute-start(bf16[400,128]{1,0:T(8,128)(2,1)} %get-tuple-element.71), channel_id=1, source_target_pairs={{64,0},{128,1},{192,64},{0,65},{65,128},{129,129},{193,192},{1,193... | collective-permute-start | bytes 307208 | tf_op jit(solution)/shard_map/ppermute | solution.py:59
  265.5 2.0 copy-start.13
  265.5 10.9 %collective-permute-start.31 = (bf16[400,128]{1,0:T(8,128)(2,1)}, bf16[400,128]{1,0:T(8,128)(2,1)S(1)}, u32[]{:S(2)}, u32[]{:S(2)}) collective-permute-start(bf16[400,128]{1,0:T(8,128)(2,1)} %get-tuple-element.70), channel_id=1, source_target_pairs={{0,0},{64,1},{128,64},{192,65},{1,128},{65,129},{129,192},{193,193... | collective-permute-start | bytes 307208 | tf_op jit(solution)/shard_map/ppermute | solution.py:59
  267.5 0.7 copy-start.14
where the time goes:
time: 279 us; the launch traced here: 278 us
  waiting for transfers between devices  96.3 us (35%)
  starting transfers between devices  93.5 us (34%)
  Pallas kernels  67.7 us (24%)
  local copies, waits for them, and re-layouts  16.1 us (6%)
  other arithmetic  3.12 us (1%)
    pallas_call x12, Pallas kernels, call(): pl.pallas_call(body, out_shape=[jax.ShapeDtypeStruct(s, d) for s, d in ou...  67.7 us
    ppermute x26, waiting for transfers between devices, shift(): return lax.ppermute(v, axis, [(i, (i + by) % n) for i in range(n)])  56.9 us
    ppermute x26, starting transfers between devices, shift(): return lax.ppermute(v, axis, [(i, (i + by) % n) for i in range(n)])  33.8 us
    ppermute x8, starting transfers between devices, from_core(): return lax.ppermute(v, ('zh', 'c'), pairs)  33.4 us
    ppermute x4, starting transfers between devices, to_core(): return lax.ppermute(v, ('zh', 'c'), pairs)  16.3 us
    ppermute x8, waiting for transfers between devices, from_core(): return lax.ppermute(v, ('zh', 'c'), pairs)  15.3 us
    all_to_all x2, waiting for transfers between devices, scatter_rows(): lax.all_to_all(part, 'x', 0, 0)  12.8 us
    ppermute x4, waiting for transfers between devices, to_core(): return lax.ppermute(v, ('zh', 'c'), pairs)  11.4 us
  transfers between devices with their start and end apart: 40, of which 15 were waited for; matrix products, arithmetic and copies ran while one was open for 3% of the time, Pallas kernels for 18%

commit v1 on v0

--- a/solution.py
+++ b/solution.py
@@ -39,6 +39,14 @@
 def shift(v, axis, by):
     n = SIZES[axis]
     return lax.ppermute(v, axis, [(i, (i + by) % n) for i in range(n)])
+
+
+def to_far_side(v):
+    pairs = []
+    for zh in range(4):
+        pairs.append((zh * 2, (zh + 3) % 4 * 2 + 1))
+        pairs.append((zh * 2 + 1, (zh + 1) % 4 * 2))
+    return lax.ppermute(v, ("zh", "zl"), pairs)
 
 
 def to_core(v, k):
@@ -301,11 +309,12 @@
         [pos, lax.all_to_all(part, "x", 0, 0)],
         deps=deps,
     )
+    got = jnp.concatenate([shift(send[:ROWS], "zl", 1), to_far_side(send[ROWS:])])
     blocks = call(
         split_kernel,
         [((ROWS + extra, 128), BF16)] * 4,
         1,
-        [pos, keep, shift(send, "zl", 1)],
+        [pos, keep, got],
         [pltpu.VMEM((rows, 256), F32)],
         deps=split_deps,
     )
@@ -333,7 +342,10 @@
     got = [to_core(msg, k) for k in range(4)]
     cnt = jnp.concatenate([g[2 * ROWS :] for g in got])
     ts = jnp.concatenate(got)
-    ts_ring = ring(jnp.concatenate([ts, shift(ts, "zl", 1)]), "x")
+    low, high = jnp.concatenate([got[3], got[0]]), jnp.concatenate(got[1:3])
+    crossing = jnp.where(lax.axis_index("zl") == 0, low, high)
+    partner = shift(jnp.concatenate(got[:2]), "zl", 1)
+    ts_ring = ring(jnp.concatenate([ts, partner, to_far_side(crossing)]), "x")
     w = call(
         pack_weights,
         [((6, 128, 128), BF16)] * 4,

time: 279 us -> 285 us (1.022)
  starting transfers between devices: 93.5 us -> 102 us
  waiting for transfers between devices: 96.3 us -> 88.7 us
    ppermute x0 -> x3, starting transfers between devices: none -> 11.8 us  [to_far_side(): return lax.ppermute(v, ('zh', 'zl'), pairs)]
    ppermute x26, waiting for transfers between devices: 56.9 us -> 48.6 us  [shift(): return lax.ppermute(v, axis, [(i, (i + by) % n) for i in range(n)])]
    ppermute x8, starting transfers between devices: 33.4 us -> 26.5 us  [from_core(): return lax.ppermute(v, ('zh', 'c'), pairs)]
    ppermute x26, starting transfers between devices: 33.8 us -> 37 us  [shift(): return lax.ppermute(v, axis, [(i, (i + by) % n) for i in range(n)])]
    slice x0 -> x3, local copies, waits for them, and re-layouts: none -> 2.95 us  [the longest x2 2 us: scatter_rows(): send[:ROWS]]
    unnamed x44 -> x41, local copies, waits for them, and re-layouts: 10.3 us -> 9.6 us
  transfers between devices with their start and end apart: 40 -> 43, of which waited for: 15 -> 18; matrix products, arithmetic and copies ran while one was open for 3% -> 5% of each run, Pallas kernels for 18% -> 16%
where the time goes in v1:
time: 285 us; the launch traced here: 282 us
  starting transfers between devices  102 us (36%)
  waiting for transfers between devices  88.7 us (31%)
  Pallas kernels  67.7 us (24%)
  local copies, waits for them, and re-layouts  18.3 us (6%)
  other arithmetic  4.75 us (2%)
    pallas_call x12, Pallas kernels, call(): pl.pallas_call(body, out_shape=[jax.ShapeDtypeStruct(s, d) for s, d in ou...  67.7 us
    ppermute x26, waiting for transfers between devices, shift(): return lax.ppermute(v, axis, [(i, (i + by) % n) for i in range(n)])  48.6 us
    ppermute x26, starting transfers between devices, shift(): return lax.ppermute(v, axis, [(i, (i + by) % n) for i in range(n)])  37 us
    ppermute x8, starting transfers between devices, from_core(): return lax.ppermute(v, ('zh', 'c'), pairs)  26.5 us
    ppermute x4, starting transfers between devices, to_core(): return lax.ppermute(v, ('zh', 'c'), pairs)  16.3 us
    ppermute x8, waiting for transfers between devices, from_core(): return lax.ppermute(v, ('zh', 'c'), pairs)  14.1 us
    all_to_all x2, waiting for transfers between devices, scatter_rows(): lax.all_to_all(part, 'x', 0, 0)  12.1 us
    ppermute x3, starting transfers between devices, to_far_side(): return lax.ppermute(v, ('zh', 'zl'), pairs)  11.8 us
  transfers between devices with their start and end apart: 43, of which 18 were waited for; matrix products, arithmetic and copies ran while one was open for 5% of the time, Pallas kernels for 16%

profile of v1, /device:TPU:91, one launch (start us, length us, event | category | flops | bytes accessed | tf_op | source)
XLA Modules:
  0.0 282.2 jit_solution(8060431564027097797)
XLA Ops:
  0.6 1.5 broadcast_in_dim.5.refs_3_
  2.1 1.8 pack_tokens.1
  3.9 6.7 %collective-permute-start.3 = (bf16[784,128]{1,0:T(8,128)(2,1)}, bf16[784,128]{1,0:T(8,128)(2,1)S(1)}, u32[]{:S(2)}, u32[]{:S(2)}) collective-permute-start(bf16[784,128]{1,0:T(8,128)(2,1)} %pack_tokens.1), channel_id=1, source_target_pairs={{0,192},{1,0},{64,64},{65,128},{128,193},{129,1},{192,65},{193,129... | collective-permute-start | bytes 602120 | tf_op jit(solution)/shard_map/ppermute | solution.py:58
  10.7 5.2 %collective-permute-start.1 = (bf16[784,128]{1,0:T(8,128)(2,1)}, bf16[784,128]{1,0:T(8,128)(2,1)S(1)}, u32[]{:S(2)}, u32[]{:S(2)}) collective-permute-start(bf16[784,128]{1,0:T(8,128)(2,1)} %pack_tokens.1), channel_id=1, source_target_pairs={{0,64},{1,128},{64,192},{65,0},{128,65},{129,129},{192,193},{193,1... | collective-permute-start | bytes 602120 | tf_op jit(solution)/shard_map/ppermute | solution.py:58
  15.9 4.4 %collective-permute-start = (bf16[784,128]{1,0:T(8,128)(2,1)}, bf16[784,128]{1,0:T(8,128)(2,1)S(1)}, u32[]{:S(2)}, u32[]{:S(2)}) collective-permute-start(bf16[784,128]{1,0:T(8,128)(2,1)} %pack_tokens.1), channel_id=1, source_target_pairs={{0,0},{1,64},{64,128},{65,192},{128,1},{129,65},{192,129},{193,193... | collective-permute-start | bytes 602120 | tf_op jit(solution)/shard_map/ppermute | solution.py:58
  20.3 2.8 collective-permute-done.2
  23.1 7.7 %collective-permute-done.1 = bf16[784,128]{1,0:T(8,128)(2,1)S(1)} collective-permute-done((bf16[784,128]{1,0:T(8,128)(2,1)}, bf16[784,128]{1,0:T(8,128)(2,1)S(1)}, u32[]{:S(2)}, u32[]{:S(2)}) %collective-permute-start.1) | collective-permute-done | bytes 200736 | tf_op jit(solution)/shard_map/ppermute | solution.py:58
  31.9 1.0 collective-permute-start.5
  35.7 5.6 %collective-permute-done.4 = bf16[1568,128]{1,0:T(8,128)(2,1)S(1)} collective-permute-done((bf16[1568,128]{1,0:T(8,128)(2,1)S(1)}, bf16[1568,128]{1,0:T(8,128)(2,1)S(1)}, u32[]{:S(2)}, u32[]{:S(2)}) %collective-permute-start.4) | collective-permute-done | bytes 401440 | tf_op jit(solution)/shard_map/ppermute | solution.py:41
  43.0 1.2 collective-permute-start.6
  45.1 2.2 pack_weights.1
  47.3 2.6 collective-permute-start.12
  49.8 3.3 %collective-permute-start.10 = (bf16[6,128,128]{2,1,0:T(8,128)(2,1)}, bf16[6,128,128]{2,1,0:T(8,128)(2,1)S(1)}, u32[]{:S(2)}, u32[]{:S(2)}) collective-permute-start(bf16[6,128,128]{2,1,0:T(8,128)(2,1)} %get-tuple-element.44), channel_id=1, source_target_pairs={{0,64},{64,128},{128,192},{192,0},{1,65},{65,129},{129,193},{193,1... | collective-permute-start | bytes 589832 | tf_op jit(solution)/shard_map/ppermute | solution.py:41
  53.1 1.1 collective-permute-done.12
  54.2 7.9 %collective-permute-done.11 = bf16[6,128,128]{2,1,0:T(8,128)(2,1)S(1)} collective-permute-done((bf16[6,128,128]{2,1,0:T(8,128)(2,1)}, bf16[6,128,128]{2,1,0:T(8,128)(2,1)S(1)}, u32[]{:S(2)}, u32[]{:S(2)}) %collective-permute-start.11) | collective-permute-done | bytes 196640 | tf_op jit(solution)/shard_map/ppermute | solution.py:41
  62.1 1.1 collective-permute-done.10
  63.2 1.0 pad_maximum_fusion.refs_3_
  64.3 1.5 collective-permute-start.14
  65.8 11.8 %collective-permute-done.6.refs_2_ = bf16[6272,128]{1,0:T(8,128)(2,1)S(1)} collective-permute-done((bf16[6272,128]{1,0:T(8,128)(2,1)}, bf16[6272,128]{1,0:T(8,128)(2,1)S(1)}, u32[]{:S(2)}, u32[]{:S(2)}) %collective-permute-start.6) | collective-permute-done | bytes 1605664 | tf_op jit(solution)/shard_map/ppermute | solution.py:41
  77.7 1.3 collective-permute-start.8
  79.1 1.2 collective-permute-start.9
  80.2 1.0 slice.59
  81.4 1.0 slice.60
  82.4 1.5 collective-permute-start.16
  83.9 4.7 %collective-permute-start.17 = (bf16[4,6,128,128]{3,2,1,0:T(8,128)(2,1)S(1)}, bf16[4,6,128,128]{3,2,1,0:T(8,128)(2,1)S(1)}, u32[]{:S(2)}, u32[]{:S(2)}) collective-permute-start(bf16[4,6,128,128]{3,2,1,0:T(8,128)(2,1)S(1)} %pad_maximum_fusion.refs_3_), channel_id=1, source_target_pairs={{0,1},{1,0},{2,3},{3,2},{4,5},{5,4},{6,7},{7,6},{8,9},{9,8},{10,11... | collective-permute-start | bytes 2359304 | tf_op jit(solution)/shard_map/ppermute | solution.py:41
  88.6 4.7 %collective-permute-start.18 = (bf16[4,6,128,128]{3,2,1,0:T(8,128)(2,1)}, bf16[4,6,128,128]{3,2,1,0:T(8,128)(2,1)S(1)}, u32[]{:S(2)}, u32[]{:S(2)}) collective-permute-start(bf16[4,6,128,128]{3,2,1,0:T(8,128)(2,1)} %collective-permute-done.13.refs_4_), channel_id=1, source_target_pairs={{0,1},{1,0},{2,3},{3,2},{4,5},{5,4},{6,7},{7,6},{8,9},{9,8},{10,11... | collective-permute-start | bytes 2359304 | tf_op jit(solution)/shard_map/ppermute | solution.py:41
  93.4 3.8 %collective-permute-start.19 = (bf16[4,6,128,128]{3,2,1,0:T(8,128)(2,1)}, bf16[4,6,128,128]{3,2,1,0:T(8,128)(2,1)}, u32[]{:S(2)}, u32[]{:S(2)}) collective-permute-start(bf16[4,6,128,128]{3,2,1,0:T(8,128)(2,1)} %collective-permute-done.14.refs_5_), channel_id=1, source_target_pairs={{0,1},{1,0},{2,3},{3,2},{4,5},{5,4},{6,7},{7,6},{8,9},{9,8},{10,11... | collective-permute-start | bytes 2359304 | tf_op jit(solution)/shard_map/ppermute | solution.py:41
  98.1 1.3 collective-permute-start.21
  100.1 5.4 %place_tokens.1.refs_2_.refs_6_ = bf16[768,2048]{1,0:T(8,128)(2,1)} custom-call(s32[5]{0:T(128)} %stack.38.refs_0_, bf16[6272,128]{1,0:T(8,128)(2,1)} %constant_dynamic-update-slice_fusion.refs_1_, bf16[6272,128]{1,0:T(8,128)(2,1)} %copy-done.2, bf16[6272,128]{1,0:T(8,128)(2,1)} %copy-done.3, bf16[3136,128]{1,0:T(8,128)(2,1)} %copy-done.7, ...), custom_call_target="tpu_custom_call" | custom-call | tf_op jit(solution)/shard_map/place_tokens/pallas_call | solution.py:23
  107.5 14.6 %forward_kernel.1 = (bf16[2048,1024]{1,0:T(8,128)(2,1)}, bf16[512,2048]{1,0:T(8,128)(2,1)}, f32[768,256]{1,0:T(8,128)}, f32[768,256]{1,0:T(8,128)}, f32[2,768,12...) custom-call(s32[5]{0:T(128)} %stack.38.refs_0_, bf16[64,128]{1,0:T(8,128)(2,1)} %pad_maximum_fusion.4.refs_1_, ...), custom_call_target="tpu_custom_call" | custom-call | flops 4831838208 | bytes 31457280 | tf_op jit(solution)/shard_map/forward_kernel/pallas_call | solution.py:23
  122.1 5.4 %all-to-all-start = ((bf16[4,768,512]{2,1,0:T(8,128)(2,1)}), bf16[4,768,512]{2,1,0:T(8,128)(2,1)S(1)}, u32[]{:S(2)}, u32[]{:S(2)}) async-start(bf16[4,768,512]{2,1,0:T(8,128)(2,1)} %get-tuple-element.47), calls=%async_computation | async-start | bytes 6291456 | tf_op jit(solution)/shard_map/all_to_all | solution.py:309
  127.5 23.0 %backward_kernel.1 = (bf16[4,784,512]{2,1,0:T(8,128)(2,1)}, bf16[4,4,6,128,128]{4,3,2,1,0:T(8,128)(2,1)}, bf16[4,4,6,128,128]{4,3,2,1,0:T(8,128)(2,1)}) custom-call(s32[5]{0:T(128)} %stack.38.refs_0_, bf16[6272,128]{1,0:T(8,128)(2,1)} %constant_dynamic-update-slice_fusion.refs_1_, bf16[6272,128]{1,0:T(8,128)(2,1)} %copy-done.2, bf16[6272,128]{1,0:T(8,128)(2,1)} %copy-done.3, ...), custom_call_target="tpu_custom_call" | custom-call | flops 9663676416 | bytes 31457280 | tf_op jit(solution)/shard_map/backward_kernel/pallas_call | solution.py:23
  151.4 12.1 %all-to-all-done.refs_1_ = bf16[4,768,512]{2,1,0:T(8,128)(2,1)S(1)} async-done(((bf16[4,768,512]{2,1,0:T(8,128)(2,1)}), bf16[4,768,512]{2,1,0:T(8,128)(2,1)S(1)}, u32[]{:S(2)}, u32[]{:S(2)}) %all-to-all-start) | async-done | bytes 3145760 | tf_op jit(solution)/shard_map/all_to_all | solution.py:309
  163.5 1.7 copy-done.1
  165.1 4.9 %all-to-all-start.1 = ((bf16[4,784,512]{2,1,0:T(8,128)(2,1)}), bf16[4,784,512]{2,1,0:T(8,128)(2,1)S(1)}, u32[]{:S(2)}, u32[]{:S(2)}) async-start(bf16[4,784,512]{2,1,0:T(8,128)(2,1)} %get-tuple-element.63), calls=%async_computation.1 | async-start | bytes 6422528 | tf_op jit(solution)/shard_map/all_to_all | solution.py:309
  170.0 4.8 %add_cores_kernel.1 = (bf16[4,6,128,128]{3,2,1,0:T(8,128)(2,1)}, bf16[4,6,128,128]{3,2,1,0:T(8,128)(2,1)}, bf16[4,6,128,128]{3,2,1,0:T(8,128)(2,1)}, bf16[4,6,128,128]{3,2,1,0:T(8,128)(2,1)}) custom-call(bf16[4,4,6,128,128]{4,3,2,1,0:T(8,128)(2,1)} %get-tuple-element.54.refs_0_, bf16[4,4,6,128,128]{4,3,2,1,0:T(8,128)(2,1)} %collective-permute-done.22.refs_1_), custom_call_target="tpu_custom_call" | custom-call | tf_op jit(solution)/shard_map/add_cores_kernel/pallas_call | solution.py:23
  174.8 3.3 %sum_x_kernel.2 = (f32[768,256]{1,0:T(8,128)}, bf16[768,256]{1,0:T(8,128)(2,1)}) custom-call(s32[5]{0:T(128)} %stack.38.refs_0_, bf16[4,768,512]{2,1,0:T(8,128)(2,1)} %copy-done.1, bf16[4,6,128,128]{3,2,1,0:T(8,128)(2,1)} %get-tuple-element.56.refs_2_.refs_0_), custom_call_target="tpu_custom_call" | custom-call | tf_op jit(solution)/shard_map/sum_x_kernel/pallas_call | solution.py:23
  178.0 1.1 fusion
  179.1 10.7 %collective-permute-start.24 = (bf16[384,256]{1,0:T(8,128)(2,1)S(1)}, bf16[384,256]{1,0:T(8,128)(2,1)S(1)}, u32[]{:S(2)}, u32[]{:S(2)}) collective-permute-start(bf16[384,256]{1,0:T(8,128)(2,1)S(1)} %get-tuple-element.83), channel_id=1, source_target_pairs={{0,194},{2,64},{64,2},{66,128},{128,66},{130,192},{192,130},{194,0... | collective-permute-start | bytes 589832 | tf_op jit(solution)/shard_map/ppermute | solution.py:49
  191.3 2.4 collective-permute-done.24
  195.4 2.1 split_kernel.2
  197.5 4.5 %collective-permute-start.28 = (bf16[384,128]{1,0:T(8,128)(2,1)}, bf16[384,128]{1,0:T(8,128)(2,1)S(1)}, u32[]{:S(2)}, u32[]{:S(2)}) collective-permute-start(bf16[384,128]{1,0:T(8,128)(2,1)} %get-tuple-element.62), channel_id=1, source_target_pairs={{192,0},{0,1},{64,64},{128,65},{193,128},{1,129},{65,192},{129,193... | collective-permute-start | bytes 294920 | tf_op jit(solution)/shard_map/ppermute | solution.py:67
  202.0 3.4 %collective-permute-start.27 = (bf16[384,128]{1,0:T(8,128)(2,1)}, bf16[384,128]{1,0:T(8,128)(2,1)S(1)}, u32[]{:S(2)}, u32[]{:S(2)}) collective-permute-start(bf16[384,128]{1,0:T(8,128)(2,1)} %get-tuple-element.61), channel_id=1, source_target_pairs={{128,0},{192,1},{0,64},{64,65},{129,128},{193,129},{1,192},{65,193... | collective-permute-start | bytes 294920 | tf_op jit(solution)/shard_map/ppermute | solution.py:67
  205.4 1.8 collective-permute-done.28
  207.2 6.0 %collective-permute-start.26 = (bf16[384,128]{1,0:T(8,128)(2,1)}, bf16[384,128]{1,0:T(8,128)(2,1)S(1)}, u32[]{:S(2)}, u32[]{:S(2)}) collective-permute-start(bf16[384,128]{1,0:T(8,128)(2,1)} %get-tuple-element.60), channel_id=1, source_target_pairs={{64,0},{128,1},{192,64},{0,65},{65,128},{129,129},{193,192},{1,193... | collective-permute-start | bytes 294920 | tf_op jit(solution)/shard_map/ppermute | solution.py:67
  213.2 1.9 collective-permute-start.25
  215.1 8.1 %collective-permute-done.25 = bf16[384,128]{1,0:T(8,128)(2,1)S(1)} collective-permute-done((bf16[384,128]{1,0:T(8,128)(2,1)}, bf16[384,128]{1,0:T(8,128)(2,1)S(1)}, u32[]{:S(2)}, u32[]{:S(2)}) %collective-permute-start.25) | collective-permute-done | bytes 98336 | tf_op jit(solution)/shard_map/ppermute | solution.py:67
  224.0 1.7 copy-done
  225.7 3.3 %sum_x_kernel.3 = (f32[784,256]{1,0:T(8,128)}, bf16[784,256]{1,0:T(8,128)(2,1)}) custom-call(s32[5]{0:T(128)} %stack.38.refs_0_, bf16[4,784,512]{2,1,0:T(8,128)(2,1)} %copy-done, bf16[384,128]{1,0:T(8,128)(2,1)} %multiply_convert_fusion.refs_2_), custom_call_target="tpu_custom_call" | custom-call | tf_op jit(solution)/shard_map/sum_x_kernel/pallas_call | solution.py:23
  228.9 0.9 slice.51
  230.0 0.9 slice.50
  231.0 6.5 %collective-permute-done.29 = bf16[384,256]{1,0:T(8,128)(2,1)S(1)} collective-permute-done((bf16[384,256]{1,0:T(8,128)(2,1)S(1)}, bf16[384,256]{1,0:T(8,128)(2,1)S(1)}, u32[]{:S(2)}, u32[]{:S(2)}) %collective-permute-start.29) | collective-permute-done | bytes 196640 | tf_op jit(solution)/shard_map/ppermute | solution.py:41
  238.3 2.9 %sum_y_kernel.1 = (bf16[6,128,128]{2,1,0:T(8,128)(2,1)}, bf16[6,128,128]{2,1,0:T(8,128)(2,1)}, bf16[6,128,128]{2,1,0:T(8,128)(2,1)}, bf16[6,128,128]{2,1,0:T(8,128)(2,1)}) custom-call(bf16[4,6,128,128]{3,2,1,0:T(8,128)(2,1)} %get-tuple-element.56.refs_2_.refs_0_, bf16[4,6,128,128]{3,2,1,0:T(8,128)(2,1)} %collective-permute-done.31.refs_1_, ...), custom_call_target="tpu_custom_call" | custom-call | tf_op jit(solution)/shard_map/sum_y_kernel/pallas_call | solution.py:23
  241.2 2.1 split_kernel.3
  243.4 2.6 collective-permute-start.37
  245.9 4.3 %collective-permute-start.36 = (bf16[400,128]{1,0:T(8,128)(2,1)}, bf16[400,128]{1,0:T(8,128)(2,1)S(1)}, u32[]{:S(2)}, u32[]{:S(2)}) collective-permute-start(bf16[400,128]{1,0:T(8,128)(2,1)} %get-tuple-element.72), channel_id=1, source_target_pairs={{128,0},{192,1},{0,64},{64,65},{129,128},{193,129},{1,192},{65,193... | collective-permute-start | bytes 307208 | tf_op jit(solution)/shard_map/ppermute | solution.py:67
  250.2 1.9 collective-permute-start.35
  252.1 1.9 collective-permute-start.34
  254.1 2.2 collective-permute-start.38
  256.3 3.9 %collective-permute-start.39 = (bf16[6,128,128]{2,1,0:T(8,128)(2,1)}, bf16[6,128,128]{2,1,0:T(8,128)(2,1)S(1)}, u32[]{:S(2)}, u32[]{:S(2)}) collective-permute-start(bf16[6,128,128]{2,1,0:T(8,128)(2,1)} %get-tuple-element.75), channel_id=1, source_target_pairs={{0,128},{64,192},{128,0},{192,64},{1,129},{65,193},{129,1},{193,65... | collective-permute-start | bytes 589832 | tf_op jit(solution)/shard_map/ppermute | solution.py:41
  260.1 4.2 %collective-permute-done.34 = bf16[400,128]{1,0:T(8,128)(2,1)S(1)} collective-permute-done((bf16[400,128]{1,0:T(8,128)(2,1)}, bf16[400,128]{1,0:T(8,128)(2,1)S(1)}, u32[]{:S(2)}, u32[]{:S(2)}) %collective-permute-start.34) | collective-permute-done | bytes 102432 | tf_op jit(solution)/shard_map/ppermute | solution.py:67
  265.7 3.4 %collective-permute-done.38.refs_2_ = bf16[6,128,128]{2,1,0:T(8,128)(2,1)S(1)} collective-permute-done((bf16[6,128,128]{2,1,0:T(8,128)(2,1)}, bf16[6,128,128]{2,1,0:T(8,128)(2,1)S(1)}, u32[]{:S(2)}, u32[]{:S(2)}) %collective-permute-start.38) | collective-permute-done | bytes 196640 | tf_op jit(solution)/shard_map/ppermute | solution.py:41
  269.0 9.5 %collective-permute-done.39.refs_3_ = bf16[6,128,128]{2,1,0:T(8,128)(2,1)S(1)} collective-permute-done((bf16[6,128,128]{2,1,0:T(8,128)(2,1)}, bf16[6,128,128]{2,1,0:T(8,128)(2,1)S(1)}, u32[]{:S(2)}, u32[]{:S(2)}) %collective-permute-start.39) | collective-permute-done | bytes 196640 | tf_op jit(solution)/shard_map/ppermute | solution.py:41
  280.0 2.2 finish_kernel.1
  (101 shorter events, 19.0 us)
Async XLA Ops:
  3.9 16.4 %collective-permute-start.3 = (bf16[784,128]{1,0:T(8,128)(2,1)}, bf16[784,128]{1,0:T(8,128)(2,1)S(1)}, u32[]{:S(2)}, u32[]{:S(2)}) collective-permute-start(bf16[784,128]{1,0:T(8,128)(2,1)} %pack_tokens.1), channel_id=1, source_target_pairs={{0,192},{1,0},{64,64},{65,128},{128,193},{129,1},{192,65},{193,129... | collective-permute-start | bytes 602120 | tf_op jit(solution)/shard_map/ppermute | solution.py:58
  10.6 12.5 %collective-permute-start.2 = (bf16[784,128]{1,0:T(8,128)(2,1)}, bf16[784,128]{1,0:T(8,128)(2,1)S(1)}, u32[]{:S(2)}, u32[]{:S(2)}) collective-permute-start(bf16[784,128]{1,0:T(8,128)(2,1)} %pack_tokens.1), channel_id=1, source_target_pairs={{0,128},{1,192},{64,0},{65,64},{128,129},{129,193},{192,1},{193,65... | collective-permute-start | bytes 602120 | tf_op jit(solution)/shard_map/ppermute | solution.py:58
  10.7 20.1 %collective-permute-start.1 = (bf16[784,128]{1,0:T(8,128)(2,1)}, bf16[784,128]{1,0:T(8,128)(2,1)S(1)}, u32[]{:S(2)}, u32[]{:S(2)}) collective-permute-start(bf16[784,128]{1,0:T(8,128)(2,1)} %pack_tokens.1), channel_id=1, source_target_pairs={{0,64},{1,128},{64,192},{65,0},{128,65},{129,129},{192,193},{193,1... | collective-permute-start | bytes 602120 | tf_op jit(solution)/shard_map/ppermute | solution.py:58
  15.9 15.8 %collective-permute-start = (bf16[784,128]{1,0:T(8,128)(2,1)}, bf16[784,128]{1,0:T(8,128)(2,1)S(1)}, u32[]{:S(2)}, u32[]{:S(2)}) collective-permute-start(bf16[784,128]{1,0:T(8,128)(2,1)} %pack_tokens.1), channel_id=1, source_target_pairs={{0,0},{1,64},{64,128},{65,192},{128,1},{129,65},{192,129},{193,193... | collective-permute-start | bytes 602120 | tf_op jit(solution)/shard_map/ppermute | solution.py:58
  23.1 12.6 %copy-start.4 = (bf16[784,128]{1,0:T(8,128)(2,1)}, bf16[784,128]{1,0:T(8,128)(2,1)S(1)}, u32[]{:S(2)}) copy-start(bf16[784,128]{1,0:T(8,128)(2,1)S(1)} %collective-permute-done.2) | copy-start | bytes 602116
  30.8 4.9 %copy-start.5 = (bf16[784,128]{1,0:T(8,128)(2,1)}, bf16[784,128]{1,0:T(8,128)(2,1)S(1)}, u32[]{:S(2)}) copy-start(bf16[784,128]{1,0:T(8,128)(2,1)S(1)} %collective-permute-done.1) | copy-start | bytes 602116
  31.7 4.0 %copy-start.6 = (bf16[784,128]{1,0:T(8,128)(2,1)}, bf16[784,128]{1,0:T(8,128)(2,1)S(1)}, u32[]{:S(2)}) copy-start(bf16[784,128]{1,0:T(8,128)(2,1)S(1)} %collective-permute-done) | copy-start | bytes 602116
  31.8 9.5 %collective-permute-start.4 = (bf16[1568,128]{1,0:T(8,128)(2,1)S(1)}, bf16[1568,128]{1,0:T(8,128)(2,1)S(1)}, u32[]{:S(2)}, u32[]{:S(2)}) collective-permute-start(bf16[1568,128]{1,0:T(8,128)(2,1)S(1)} %get-tuple-element.81), channel_id=1, source_target_pairs={{0,2},{2,0},{1,3},{3,1},{4,6},{6,4},{5,7},{7,5},{8,10},{10,8},{9,1... | collective-permute-start | bytes 1204232 | tf_op jit(solution)/shard_map/ppermute | solution.py:41
  31.9 10.2 %collective-permute-start.5 = (bf16[1568,128]{1,0:T(8,128)(2,1)S(1)}, bf16[1568,128]{1,0:T(8,128)(2,1)S(1)}, u32[]{:S(2)}, u32[]{:S(2)}) collective-permute-start(bf16[1568,128]{1,0:T(8,128)(2,1)S(1)} %get-tuple-element.80), channel_id=1, source_target_pairs={{0,194},{2,64},{64,2},{66,128},{128,66},{130,192},{192,130},{194,0... | collective-permute-start | bytes 1204232 | tf_op jit(solution)/shard_map/ppermute | solution.py:49
  43.0 34.6 %collective-permute-start.6 = (bf16[6272,128]{1,0:T(8,128)(2,1)}, bf16[6272,128]{1,0:T(8,128)(2,1)S(1)}, u32[]{:S(2)}, u32[]{:S(2)}) collective-permute-start(bf16[6272,128]{1,0:T(8,128)(2,1)} %constant_dynamic-update-slice_fusion.refs_1_), channel_id=1, source_target_pairs={{0,4},{4,8},{8,12},{12,0},{1,5},{5,9},{9,13},{13,1},{2,6},{6,10},{... | collective-permute-start | bytes 4816904 | tf_op jit(solution)/shard_map/ppermute | solution.py:41
  44.2 34.8 %collective-permute-start.7 = (bf16[6272,128]{1,0:T(8,128)(2,1)}, bf16[6272,128]{1,0:T(8,128)(2,1)S(1)}, u32[]{:S(2)}, u32[]{:S(2)}) collective-permute-start(bf16[6272,128]{1,0:T(8,128)(2,1)} %constant_dynamic-update-slice_fusion.refs_1_), channel_id=1, source_target_pairs={{0,12},{4,0},{8,4},{12,8},{1,13},{5,1},{9,5},{13,9},{2,14},{6,2},{... | collective-permute-start | bytes 4816904 | tf_op jit(solution)/shard_map/ppermute | solution.py:41
  47.3 6.9 %collective-permute-start.12 = (bf16[6,128,128]{2,1,0:T(8,128)(2,1)}, bf16[6,128,128]{2,1,0:T(8,128)(2,1)S(1)}, u32[]{:S(2)}, u32[]{:S(2)}) collective-permute-start(bf16[6,128,128]{2,1,0:T(8,128)(2,1)} %get-tuple-element.46), channel_id=1, source_target_pairs={{0,192},{64,0},{128,64},{192,128},{1,193},{65,1},{129,65},{193,129... | collective-permute-start | bytes 589832 | tf_op jit(solution)/shard_map/ppermute | solution.py:41
  49.8 12.3 %collective-permute-start.11 = (bf16[6,128,128]{2,1,0:T(8,128)(2,1)}, bf16[6,128,128]{2,1,0:T(8,128)(2,1)S(1)}, u32[]{:S(2)}, u32[]{:S(2)}) collective-permute-start(bf16[6,128,128]{2,1,0:T(8,128)(2,1)} %get-tuple-element.45), channel_id=1, source_target_pairs={{0,128},{64,192},{128,0},{192,64},{1,129},{65,193},{129,1},{193,65... | collective-permute-start | bytes 589832 | tf_op jit(solution)/shard_map/ppermute | solution.py:41
  49.8 13.3 %collective-permute-start.10 = (bf16[6,128,128]{2,1,0:T(8,128)(2,1)}, bf16[6,128,128]{2,1,0:T(8,128)(2,1)S(1)}, u32[]{:S(2)}, u32[]{:S(2)}) collective-permute-start(bf16[6,128,128]{2,1,0:T(8,128)(2,1)} %get-tuple-element.44), channel_id=1, source_target_pairs={{0,64},{64,128},{128,192},{192,0},{1,65},{65,129},{129,193},{193,1... | collective-permute-start | bytes 589832 | tf_op jit(solution)/shard_map/ppermute | solution.py:41
  64.2 19.7 %copy-start.9 = (bf16[4,6,128,128]{3,2,1,0:T(8,128)(2,1)}, bf16[4,6,128,128]{3,2,1,0:T(8,128)(2,1)S(1)}, u32[]{:S(2)}) copy-start(bf16[4,6,128,128]{3,2,1,0:T(8,128)(2,1)S(1)} %pad_maximum_fusion.refs_3_) | copy-start | bytes 2359300
  64.2 16.0 %collective-permute-start.13 = (bf16[4,6,128,128]{3,2,1,0:T(8,128)(2,1)S(1)}, bf16[4,6,128,128]{3,2,1,0:T(8,128)(2,1)}, u32[]{:S(2)}, u32[]{:S(2)}) collective-permute-start(bf16[4,6,128,128]{3,2,1,0:T(8,128)(2,1)S(1)} %pad_maximum_fusion.refs_3_), channel_id=1, source_target_pairs={{0,16},{16,32},{32,48},{48,0},{1,17},{17,33},{33,49},{49,1},{2,18}... | collective-permute-start | bytes 2359304 | tf_op jit(solution)/shard_map/ppermute | solution.py:41
  64.3 17.0 %collective-permute-start.14 = (bf16[4,6,128,128]{3,2,1,0:T(8,128)(2,1)S(1)}, bf16[4,6,128,128]{3,2,1,0:T(8,128)(2,1)}, u32[]{:S(2)}, u32[]{:S(2)}) collective-permute-start(bf16[4,6,128,128]{3,2,1,0:T(8,128)(2,1)S(1)} %pad_maximum_fusion.refs_3_), channel_id=1, source_target_pairs={{0,48},{16,0},{32,16},{48,32},{1,49},{17,1},{33,17},{49,33},{2,50}... | collective-permute-start | bytes 2359304 | tf_op jit(solution)/shard_map/ppermute | solution.py:41
  77.6 1.4 copy-start.2
  77.7 21.8 %slice-start = ((bf16[784,128]{1,0:T(8,128)(2,1)}), bf16[16,128]{1,0:T(8,128)(2,1)S(1)}, s32[]{:S(2)}) async-start(bf16[784,128]{1,0:T(8,128)(2,1)} %copy-done.4), calls=%async_computation.2 | async-start | bytes 8192 | tf_op jit(solution)/shard_map/slice | solution.py:343
  77.7 21.8 %slice-start.1 = ((bf16[784,128]{1,0:T(8,128)(2,1)}), bf16[16,128]{1,0:T(8,128)(2,1)S(1)}, s32[]{:S(2)}) async-start(bf16[784,128]{1,0:T(8,128)(2,1)} %copy-done.5), calls=%async_computation.3 | async-start | bytes 8192 | tf_op jit(solution)/shard_map/slice | solution.py:343
  77.7 21.8 %slice-start.2 = ((bf16[784,128]{1,0:T(8,128)(2,1)}), bf16[16,128]{1,0:T(8,128)(2,1)S(1)}, s32[]{:S(2)}) async-start(bf16[784,128]{1,0:T(8,128)(2,1)} %copy-done.6), calls=%async_computation.4 | async-start | bytes 8192 | tf_op jit(solution)/shard_map/slice | solution.py:343
  77.7 19.5 %collective-permute-start.8 = (bf16[3136,128]{1,0:T(8,128)(2,1)S(1)}, bf16[3136,128]{1,0:T(8,128)(2,1)S(1)}, u32[]{:S(2)}, u32[]{:S(2)}) collective-permute-start(bf16[3136,128]{1,0:T(8,128)(2,1)S(1)} %slice.57), channel_id=1, source_target_pairs={{0,4},{4,8},{8,12},{12,0},{1,5},{5,9},{9,13},{13,1},{2,6},{6,10},{... | collective-permute-start | bytes 2408456 | tf_op jit(solution)/shard_map/ppermute | solution.py:41
  79.0 21.1 %copy-start.3 = (bf16[6272,128]{1,0:T(8,128)(2,1)}, bf16[6272,128]{1,0:T(8,128)(2,1)S(1)}, u32[]{:S(2)}) copy-start(bf16[6272,128]{1,0:T(8,128)(2,1)S(1)} %collective-permute-done.7.refs_3_) | copy-start | bytes 4816900
  79.1 19.0 %collective-permute-start.9 = (bf16[3136,128]{1,0:T(8,128)(2,1)S(1)}, bf16[3136,128]{1,0:T(8,128)(2,1)S(1)}, u32[]{:S(2)}, u32[]{:S(2)}) collective-permute-start(bf16[3136,128]{1,0:T(8,128)(2,1)S(1)} %slice.58), channel_id=1, source_target_pairs={{0,12},{4,0},{8,4},{12,8},{1,13},{5,1},{9,5},{13,9},{2,14},{6,2},{... | collective-permute-start | bytes 2408456 | tf_op jit(solution)/shard_map/ppermute | solution.py:41
  81.3 7.3 %collective-permute-start.15 = (bf16[2,6,128,128]{3,2,1,0:T(8,128)(2,1)S(1)}, bf16[2,6,128,128]{3,2,1,0:T(8,128)(2,1)}, u32[]{:S(2)}, u32[]{:S(2)}) collective-permute-start(bf16[2,6,128,128]{3,2,1,0:T(8,128)(2,1)S(1)} %slice.59), channel_id=1, source_target_pairs={{0,16},{16,32},{32,48},{48,0},{1,17},{17,33},{33,49},{49,1},{2,18}... | collective-permute-start | bytes 1179656 | tf_op jit(solution)/shard_map/ppermute | solution.py:41
  82.4 11.0 %collective-permute-start.16 = (bf16[2,6,128,128]{3,2,1,0:T(8,128)(2,1)S(1)}, bf16[2,6,128,128]{3,2,1,0:T(8,128)(2,1)}, u32[]{:S(2)}, u32[]{:S(2)}) collective-permute-start(bf16[2,6,128,128]{3,2,1,0:T(8,128)(2,1)S(1)} %slice.60), channel_id=1, source_target_pairs={{0,48},{16,0},{32,16},{48,32},{1,49},{17,1},{33,17},{49,33},{2,50}... | collective-permute-start | bytes 1179656 | tf_op jit(solution)/shard_map/ppermute | solution.py:41
  83.9 21.6 %collective-permute-start.17 = (bf16[4,6,128,128]{3,2,1,0:T(8,128)(2,1)S(1)}, bf16[4,6,128,128]{3,2,1,0:T(8,128)(2,1)S(1)}, u32[]{:S(2)}, u32[]{:S(2)}) collective-permute-start(bf16[4,6,128,128]{3,2,1,0:T(8,128)(2,1)S(1)} %pad_maximum_fusion.refs_3_), channel_id=1, source_target_pairs={{0,1},{1,0},{2,3},{3,2},{4,5},{5,4},{6,7},{7,6},{8,9},{9,8},{10,11... | collective-permute-start | bytes 2359304 | tf_op jit(solution)/shard_map/ppermute | solution.py:41
  88.6 16.9 %collective-permute-start.18 = (bf16[4,6,128,128]{3,2,1,0:T(8,128)(2,1)}, bf16[4,6,128,128]{3,2,1,0:T(8,128)(2,1)S(1)}, u32[]{:S(2)}, u32[]{:S(2)}) collective-permute-start(bf16[4,6,128,128]{3,2,1,0:T(8,128)(2,1)} %collective-permute-done.13.refs_4_), channel_id=1, source_target_pairs={{0,1},{1,0},{2,3},{3,2},{4,5},{5,4},{6,7},{7,6},{8,9},{9,8},{10,11... | collective-permute-start | bytes 2359304 | tf_op jit(solution)/shard_map/ppermute | solution.py:41
  93.4 12.2 %collective-permute-start.19 = (bf16[4,6,128,128]{3,2,1,0:T(8,128)(2,1)}, bf16[4,6,128,128]{3,2,1,0:T(8,128)(2,1)}, u32[]{:S(2)}, u32[]{:S(2)}) collective-permute-start(bf16[4,6,128,128]{3,2,1,0:T(8,128)(2,1)} %collective-permute-done.14.refs_5_), channel_id=1, source_target_pairs={{0,1},{1,0},{2,3},{3,2},{4,5},{5,4},{6,7},{7,6},{8,9},{9,8},{10,11... | collective-permute-start | bytes 2359304 | tf_op jit(solution)/shard_map/ppermute | solution.py:41
  97.2 2.9 %copy-start.7 = (bf16[3136,128]{1,0:T(8,128)(2,1)}, bf16[3136,128]{1,0:T(8,128)(2,1)S(1)}, u32[]{:S(2)}) copy-start(bf16[3136,128]{1,0:T(8,128)(2,1)S(1)} %collective-permute-done.8.refs_4_) | copy-start | bytes 2408452
  97.2 8.4 %collective-permute-start.20 = (bf16[2,6,128,128]{3,2,1,0:T(8,128)(2,1)}, bf16[2,6,128,128]{3,2,1,0:T(8,128)(2,1)S(1)}, u32[]{:S(2)}, u32[]{:S(2)}) collective-permute-start(bf16[2,6,128,128]{3,2,1,0:T(8,128)(2,1)} %collective-permute-done.15.refs_6_), channel_id=1, source_target_pairs={{0,1},{1,0},{2,3},{3,2},{4,5},{5,4},{6,7},{7,6},{8,9},{9,8},{10,11... | collective-permute-start | bytes 1179656 | tf_op jit(solution)/shard_map/ppermute | solution.py:41
  98.1 2.0 copy-start.8
  98.1 7.5 %collective-permute-start.21 = (bf16[2,6,128,128]{3,2,1,0:T(8,128)(2,1)}, bf16[2,6,128,128]{3,2,1,0:T(8,128)(2,1)S(1)}, u32[]{:S(2)}, u32[]{:S(2)}) collective-permute-start(bf16[2,6,128,128]{3,2,1,0:T(8,128)(2,1)} %collective-permute-done.16.refs_7_), channel_id=1, source_target_pairs={{0,1},{1,0},{2,3},{3,2},{4,5},{5,4},{6,7},{7,6},{8,9},{9,8},{10,11... | collective-permute-start | bytes 1179656 | tf_op jit(solution)/shard_map/ppermute | solution.py:41
  105.5 0.9 copy-start.14
  105.5 1.1 copy-start.15
  105.6 1.2 copy-start.16
  106.8 0.8 copy-start.17
  122.1 41.3 %all-to-all-start = ((bf16[4,768,512]{2,1,0:T(8,128)(2,1)}), bf16[4,768,512]{2,1,0:T(8,128)(2,1)S(1)}, u32[]{:S(2)}, u32[]{:S(2)}) async-start(bf16[4,768,512]{2,1,0:T(8,128)(2,1)} %get-tuple-element.47), calls=%async_computation | async-start | bytes 6291456 | tf_op jit(solution)/shard_map/all_to_all | solution.py:309
  150.5 19.5 %collective-permute-start.22 = (bf16[4,4,6,128,128]{4,3,2,1,0:T(8,128)(2,1)}, bf16[4,4,6,128,128]{4,3,2,1,0:T(8,128)(2,1)}, u32[]{:S(2)}, u32[]{:S(2)}) collective-permute-start(bf16[4,4,6,128,128]{4,3,2,1,0:T(8,128)(2,1)} %get-tuple-element.55), channel_id=1, source_target_pairs={{0,1},{1,0},{2,3},{3,2},{4,5},{5,4},{6,7},{7,6},{8,9},{9,8},{10,11... | collective-permute-start | bytes 9437192 | tf_op jit(solution)/shard_map/ppermute | solution.py:41
  163.5 1.7 copy-start.1
  165.1 58.9 %all-to-all-start.1 = ((bf16[4,784,512]{2,1,0:T(8,128)(2,1)}), bf16[4,784,512]{2,1,0:T(8,128)(2,1)S(1)}, u32[]{:S(2)}, u32[]{:S(2)}) async-start(bf16[4,784,512]{2,1,0:T(8,128)(2,1)} %get-tuple-element.63), calls=%async_computation.1 | async-start | bytes 6422528 | tf_op jit(solution)/shard_map/all_to_all | solution.py:309
  178.0 45.2 %copy-start.13 = (f32[384]{0:T(512)S(1)}, f32[384]{0:T(512)}, u32[]{:S(2)}) copy-start(f32[384]{0:T(512)} %param.9) | copy-start | bytes 4612
  179.1 14.6 %collective-permute-start.24 = (bf16[384,256]{1,0:T(8,128)(2,1)S(1)}, bf16[384,256]{1,0:T(8,128)(2,1)S(1)}, u32[]{:S(2)}, u32[]{:S(2)}) collective-permute-start(bf16[384,256]{1,0:T(8,128)(2,1)S(1)} %get-tuple-element.83), channel_id=1, source_target_pairs={{0,194},{2,64},{64,2},{66,128},{128,66},{130,192},{192,130},{194,0... | collective-permute-start | bytes 589832 | tf_op jit(solution)/shard_map/ppermute | solution.py:49
  189.8 4.8 %collective-permute-start.23 = (bf16[384,256]{1,0:T(8,128)(2,1)S(1)}, bf16[384,256]{1,0:T(8,128)(2,1)S(1)}, u32[]{:S(2)}, u32[]{:S(2)}) collective-permute-start(bf16[384,256]{1,0:T(8,128)(2,1)S(1)} %get-tuple-element.82), channel_id=1, source_target_pairs={{0,2},{2,0},{1,3},{3,1},{4,6},{6,4},{5,7},{7,5},{8,10},{10,8},{9,1... | collective-permute-start | bytes 589832 | tf_op jit(solution)/shard_map/ppermute | solution.py:41
  189.8 48.5 %collective-permute-start.31 = (bf16[4,6,128,128]{3,2,1,0:T(8,128)(2,1)}, bf16[4,6,128,128]{3,2,1,0:T(8,128)(2,1)}, u32[]{:S(2)}, u32[]{:S(2)}) collective-permute-start(bf16[4,6,128,128]{3,2,1,0:T(8,128)(2,1)} %get-tuple-element.66), channel_id=1, source_target_pairs={{0,16},{16,32},{32,48},{48,0},{1,17},{17,33},{33,49},{49,1},{2,18}... | collective-permute-start | bytes 2359304 | tf_op jit(solution)/shard_map/ppermute | solution.py:41
  189.8 48.5 %collective-permute-start.32 = (bf16[4,6,128,128]{3,2,1,0:T(8,128)(2,1)}, bf16[4,6,128,128]{3,2,1,0:T(8,128)(2,1)}, u32[]{:S(2)}, u32[]{:S(2)}) collective-permute-start(bf16[4,6,128,128]{3,2,1,0:T(8,128)(2,1)} %get-tuple-element.67), channel_id=1, source_target_pairs={{0,32},{16,48},{32,0},{48,16},{1,33},{17,49},{33,1},{49,17},{2,34}... | collective-permute-start | bytes 2359304 | tf_op jit(solution)/shard_map/ppermute | solution.py:41
  190.5 47.8 %collective-permute-start.33 = (bf16[4,6,128,128]{3,2,1,0:T(8,128)(2,1)}, bf16[4,6,128,128]{3,2,1,0:T(8,128)(2,1)}, u32[]{:S(2)}, u32[]{:S(2)}) collective-permute-start(bf16[4,6,128,128]{3,2,1,0:T(8,128)(2,1)} %get-tuple-element.68), channel_id=1, source_target_pairs={{0,48},{16,0},{32,16},{48,32},{1,49},{17,1},{33,17},{49,33},{2,50}... | collective-permute-start | bytes 2359304 | tf_op jit(solution)/shard_map/ppermute | solution.py:41
  197.5 9.7 %collective-permute-start.28 = (bf16[384,128]{1,0:T(8,128)(2,1)}, bf16[384,128]{1,0:T(8,128)(2,1)S(1)}, u32[]{:S(2)}, u32[]{:S(2)}) collective-permute-start(bf16[384,128]{1,0:T(8,128)(2,1)} %get-tuple-element.62), channel_id=1, source_target_pairs={{192,0},{0,1},{64,64},{128,65},{193,128},{1,129},{65,192},{129,193... | collective-permute-start | bytes 294920 | tf_op jit(solution)/shard_map/ppermute | solution.py:67
  202.0 11.2 %collective-permute-start.27 = (bf16[384,128]{1,0:T(8,128)(2,1)}, bf16[384,128]{1,0:T(8,128)(2,1)S(1)}, u32[]{:S(2)}, u32[]{:S(2)}) collective-permute-start(bf16[384,128]{1,0:T(8,128)(2,1)} %get-tuple-element.61), channel_id=1, source_target_pairs={{128,0},{192,1},{0,64},{64,65},{129,128},{193,129},{1,192},{65,193... | collective-permute-start | bytes 294920 | tf_op jit(solution)/shard_map/ppermute | solution.py:67
  207.2 7.9 %collective-permute-start.26 = (bf16[384,128]{1,0:T(8,128)(2,1)}, bf16[384,128]{1,0:T(8,128)(2,1)S(1)}, u32[]{:S(2)}, u32[]{:S(2)}) collective-permute-start(bf16[384,128]{1,0:T(8,128)(2,1)} %get-tuple-element.60), channel_id=1, source_target_pairs={{64,0},{128,1},{192,64},{0,65},{65,128},{129,129},{193,192},{1,193... | collective-permute-start | bytes 294920 | tf_op jit(solution)/shard_map/ppermute | solution.py:67
  213.2 10.1 %collective-permute-start.25 = (bf16[384,128]{1,0:T(8,128)(2,1)}, bf16[384,128]{1,0:T(8,128)(2,1)S(1)}, u32[]{:S(2)}, u32[]{:S(2)}) collective-permute-start(bf16[384,128]{1,0:T(8,128)(2,1)} %get-tuple-element.59), channel_id=1, source_target_pairs={{0,0},{64,1},{128,64},{192,65},{1,128},{65,129},{129,192},{193,193... | collective-permute-start | bytes 294920 | tf_op jit(solution)/shard_map/ppermute | solution.py:67
  224.0 1.7 copy-start
  229.9 7.6 %collective-permute-start.30 = (bf16[400,256]{1,0:T(8,128)(2,1)S(1)}, bf16[400,256]{1,0:T(8,128)(2,1)S(1)}, u32[]{:S(2)}, u32[]{:S(2)}) collective-permute-start(bf16[400,256]{1,0:T(8,128)(2,1)S(1)} %slice.51), channel_id=1, source_target_pairs={{0,194},{2,64},{64,2},{66,128},{128,66},{130,192},{192,130},{194,0... | collective-permute-start | bytes 614408 | tf_op jit(solution)/shard_map/ppermute | solution.py:49
  230.9 6.6 %collective-permute-start.29 = (bf16[384,256]{1,0:T(8,128)(2,1)S(1)}, bf16[384,256]{1,0:T(8,128)(2,1)S(1)}, u32[]{:S(2)}, u32[]{:S(2)}) collective-permute-start(bf16[384,256]{1,0:T(8,128)(2,1)S(1)} %slice.50), channel_id=1, source_target_pairs={{0,2},{2,0},{1,3},{3,1},{4,6},{6,4},{5,7},{7,5},{8,10},{10,8},{9,1... | collective-permute-start | bytes 589832 | tf_op jit(solution)/shard_map/ppermute | solution.py:41
  243.4 12.9 %collective-permute-start.37 = (bf16[400,128]{1,0:T(8,128)(2,1)}, bf16[400,128]{1,0:T(8,128)(2,1)S(1)}, u32[]{:S(2)}, u32[]{:S(2)}) collective-permute-start(bf16[400,128]{1,0:T(8,128)(2,1)} %get-tuple-element.73), channel_id=1, source_target_pairs={{192,0},{0,1},{64,64},{128,65},{193,128},{1,129},{65,192},{129,193... | collective-permute-start | bytes 307208 | tf_op jit(solution)/shard_map/ppermute | solution.py:67
  245.9 14.2 %collective-permute-start.36 = (bf16[400,128]{1,0:T(8,128)(2,1)}, bf16[400,128]{1,0:T(8,128)(2,1)S(1)}, u32[]{:S(2)}, u32[]{:S(2)}) collective-permute-start(bf16[400,128]{1,0:T(8,128)(2,1)} %get-tuple-element.72), channel_id=1, source_target_pairs={{128,0},{192,1},{0,64},{64,65},{129,128},{193,129},{1,192},{65,193... | collective-permute-start | bytes 307208 | tf_op jit(solution)/shard_map/ppermute | solution.py:67
  250.2 9.9 %collective-permute-start.35 = (bf16[400,128]{1,0:T(8,128)(2,1)}, bf16[400,128]{1,0:T(8,128)(2,1)S(1)}, u32[]{:S(2)}, u32[]{:S(2)}) collective-permute-start(bf16[400,128]{1,0:T(8,128)(2,1)} %get-tuple-element.71), channel_id=1, source_target_pairs={{64,0},{128,1},{192,64},{0,65},{65,128},{129,129},{193,192},{1,193... | collective-permute-start | bytes 307208 | tf_op jit(solution)/shard_map/ppermute | solution.py:67
  252.1 12.2 %collective-permute-start.34 = (bf16[400,128]{1,0:T(8,128)(2,1)}, bf16[400,128]{1,0:T(8,128)(2,1)S(1)}, u32[]{:S(2)}, u32[]{:S(2)}) collective-permute-start(bf16[400,128]{1,0:T(8,128)(2,1)} %get-tuple-element.70), channel_id=1, source_target_pairs={{0,0},{64,1},{128,64},{192,65},{1,128},{65,129},{129,192},{193,193... | collective-permute-start | bytes 307208 | tf_op jit(solution)/shard_map/ppermute | solution.py:67
  254.1 15.0 %collective-permute-start.38 = (bf16[6,128,128]{2,1,0:T(8,128)(2,1)}, bf16[6,128,128]{2,1,0:T(8,128)(2,1)S(1)}, u32[]{:S(2)}, u32[]{:S(2)}) collective-permute-start(bf16[6,128,128]{2,1,0:T(8,128)(2,1)} %get-tuple-element.74), channel_id=1, source_target_pairs={{0,64},{64,128},{128,192},{192,0},{1,65},{65,129},{129,193},{193,1... | collective-permute-start | bytes 589832 | tf_op jit(solution)/shard_map/ppermute | solution.py:41
  256.3 22.2 %collective-permute-start.39 = (bf16[6,128,128]{2,1,0:T(8,128)(2,1)}, bf16[6,128,128]{2,1,0:T(8,128)(2,1)S(1)}, u32[]{:S(2)}, u32[]{:S(2)}) collective-permute-start(bf16[6,128,128]{2,1,0:T(8,128)(2,1)} %get-tuple-element.75), channel_id=1, source_target_pairs={{0,128},{64,192},{128,0},{192,64},{1,129},{65,193},{129,1},{193,65... | collective-permute-start | bytes 589832 | tf_op jit(solution)/shard_map/ppermute | solution.py:41
  260.1 19.2 %collective-permute-start.40 = (bf16[6,128,128]{2,1,0:T(8,128)(2,1)}, bf16[6,128,128]{2,1,0:T(8,128)(2,1)S(1)}, u32[]{:S(2)}, u32[]{:S(2)}) collective-permute-start(bf16[6,128,128]{2,1,0:T(8,128)(2,1)} %get-tuple-element.76), channel_id=1, source_target_pairs={{0,192},{64,0},{128,64},{192,128},{1,193},{65,1},{129,65},{193,129... | collective-permute-start | bytes 589832 | tf_op jit(solution)/shard_map/ppermute | solution.py:41
  269.0 10.3 %copy-start.10 = (bf16[6,128,128]{2,1,0:T(8,128)(2,1)}, bf16[6,128,128]{2,1,0:T(8,128)(2,1)S(1)}, u32[]{:S(2)}) copy-start(bf16[6,128,128]{2,1,0:T(8,128)(2,1)S(1)} %collective-permute-done.38.refs_2_) | copy-start | bytes 589828
  278.5 0.8 copy-start.11
  279.3 0.7 copy-start.12
